TPU v7x, 256 devices: a whole 4x4x8 slice. The times are simulated.
256 devices in a mesh: ens: 8 (over y, x_lo), tile: 32 (over z, x_hi, core).
Axes of the slice: x: 4 (x_hi: 2, x_lo: 2; x = x_hi * 2 + x_lo), y: 4, z: 8, core: 2. Of those that a mesh axis runs over, the one named last changes fastest.
Arguments:
- ens_control: float32 [64, 8, 128, 1024], P('ens', None, 'tile'), may hold values from -6 to 6
- static_control: float32 [8, 128, 1024], P(None, 'tile'), may hold values from -6 to 6
- perturbations: bfloat16 [2, 64, 8, 128, 1024], P(None, 'ens', None, 'tile'), may hold values from -6 to 6
- level_sigma: float32 [8], replicated, may hold values from 0.5 to 2
- length_class: int32 [128, 1024], P('tile'), may hold values from 0 to 3
- courant_east: float32 [128, 1024], P('tile'), may hold values from -0.45 to 0.45
- courant_north: float32 [128, 1024], P('tile'), may hold values from -0.45 to 0.45
- obs_column: int32 [131072], P('tile'), may hold values from 0 to 8191
- obs_count: int32 [1024], P('tile'), may hold values from 0 to 128, as said below
- obs_value: float32 [131072], P('tile'), may hold values from -6 to 6
- obs_weight: float32 [131072], P('tile'), may hold values from 1 to 16
- obs_kernel: float32 [8, 131072], P(None, 'tile'), may hold values from 0.25 to 1.5
Outputs:
- grad_ens: float32 [64, 8, 128, 1024], P('ens', None, 'tile')
- grad_static: float32 [8, 128, 1024], P(None, 'tile')
- departures: float32 [131072], P('tile')
Inputs may be any that keep to these rules, and one draw needn't show every extreme that they name: `obs_count`: for each owner d there is a largest count in its column: in every draw one owner strip gets exactly 128 slots from every holder; the counts of one holder sum to at most 4096.
All inputs are finite; a program needn't handle non-finite values.
Results may differ from a plain program's by a relative error of at most 0.0003.
Values sent between devices are 32-bit elements; how exact they have to be, the bound alone decides.
A program may use at most 64 MiB of HBM per device.

v0:
```python
import math

import jax
import jax.numpy as jnp
from jax import lax
from jax.sharding import PartitionSpec as P

NT = 2
NDIFF = 4


BETA_ENS = 0.8
BETA_STATIC = 0.6
DIFF_BASE = 0.06


def padded(value, sides, width):
    for axis, dim in sides:
        count, length = (lax.axis_size(axis), value.shape[dim])
        up = [(i, (i + 1) % count) for i in range(count - 1)]
        down = [(j, i) for i, j in up]
        last = lax.slice_in_dim(value, length - width, length, axis=dim)
        leading = lax.slice_in_dim(value, 0, width, axis=dim)
        before = lax.ppermute(last, axis, up)
        after = lax.ppermute(leading, axis, down)
        value = jnp.concatenate([before, value, after], axis=dim)
    return value


def laplace_of(weighted):
    center = weighted[:, 1:-1]
    return (
        weighted[:, 2:]
        + weighted[:, :-2]
        + jnp.roll(center, 1, -1)
        + jnp.roll(center, -1, -1)
        - 4.0 * center
    )


def smooth(fields, diffusion_rim):
    stiffness = diffusion_rim[NDIFF:-NDIFF]
    for sweep in range(NDIFF):
        weighted = padded(stiffness * fields, (("tile", 1),), 1)
        fields = fields + stiffness * laplace_of(weighted)
    return fields


def per_device(
    ens_control,
    static_control,
    perturbations,
    level_sigma,
    length_class,
    courant_east,
    courant_north,
    obs_column,
    obs_count,
    obs_value,
    obs_weight,
    obs_kernel,
):
    members, levels, strip_rows, row_length = ens_control.shape
    tile_count = lax.axis_size("tile")
    capacity = obs_column.shape[0] // tile_count
    factor = BETA_ENS / math.sqrt(lax.axis_size("ens") * members - 1)
    diffusion = jnp.sqrt(DIFF_BASE * (length_class.astype(jnp.float32) + 1.0))
    static_first = BETA_STATIC * level_sigma[:, None, None] * static_control
    rimmed = padded(jnp.concatenate([diffusion[None], static_first], 0), (("tile", 1),), NDIFF)
    diffusion_rim = rimmed[0]
    static_rim = rimmed[1:, NDIFF - 1 : NDIFF + strip_rows + 1]
    east_plus = jnp.maximum(courant_east, 0.0)
    east_minus = jnp.minimum(courant_east, 0.0)
    north_plus = jnp.maximum(courant_north, 0.0)
    north_minus = jnp.minimum(courant_north, 0.0)
    static_second = (
        static_first
        - east_plus * (static_first - jnp.roll(static_first, 1, -1))
        - east_minus * (jnp.roll(static_first, -1, -1) - static_first)
    )
    static_second = (
        static_second
        - north_plus * (static_first - static_rim[:, :-2])
        - north_minus * (static_rim[:, 2:] - static_first)
    )
    smoothed = smooth(ens_control.reshape(members * levels, strip_rows, row_length), diffusion_rim)
    smoothed = smoothed.reshape(members, levels, strip_rows, row_length)
    partial_sum = factor * jnp.sum(perturbations.astype(jnp.float32) * smoothed[None], axis=1)
    increment = lax.psum(partial_sum, "ens") + jnp.stack([static_first, static_second])
    columns = jnp.moveaxis(increment, 1, 0).reshape(levels, NT * strip_rows * row_length)
    block_end = jnp.cumsum(obs_count)
    block_start = block_end - obs_count
    offsets = jnp.arange(capacity, dtype=jnp.int32)
    source = block_start[:, None] + offsets[None, :]
    usable = offsets[None, :] < obs_count[:, None]
    source = jnp.minimum(source, obs_column.shape[0] - 1)
    column_blocks = jnp.where(usable, obs_column[source], -1)
    value_blocks = obs_value[source]
    weight_blocks = jnp.where(usable, obs_weight[source], 0.0)
    kernel_blocks = jnp.moveaxis(obs_kernel[:, source], 1, 0)
    owned_columns = lax.all_to_all(column_blocks, "tile", split_axis=0, concat_axis=0, tiled=True)
    owned_index = jnp.maximum(owned_columns, 0)
    owned_profile = jnp.moveaxis(columns[:, owned_index], 1, 0)
    profile_blocks = lax.all_to_all(owned_profile, "tile", split_axis=0, concat_axis=0, tiled=True)
    evolved = jnp.sum(kernel_blocks * profile_blocks, axis=1)
    departure_blocks = jnp.where(usable, weight_blocks * (evolved - value_blocks), 0.0)
    owned_partial = lax.all_to_all(
        kernel_blocks * departure_blocks[:, None], "tile", split_axis=0, concat_axis=0, tiled=True
    )
    departures = (
        jnp.zeros(obs_column.shape, jnp.float32)
        .at[source]
        .add(jnp.where(usable, departure_blocks, 0.0))
    )
    adjoint = (
        jnp.zeros(columns.shape, jnp.float32)
        .at[:, owned_index]
        .add(jnp.moveaxis(owned_partial, 1, 0))
    )
    adjoint = jnp.moveaxis(adjoint.reshape(levels, NT, strip_rows, row_length), 0, 1)
    later = adjoint[1]
    wind_terms = padded(
        jnp.concatenate([north_plus * later, north_minus * later], 0), (("tile", 1),), 1
    )
    transported = later * (1.0 - east_plus + east_minus - north_plus + north_minus)
    transported = (
        transported + jnp.roll(east_plus * later, -1, -1) - jnp.roll(east_minus * later, 1, -1)
    )
    transported = transported + wind_terms[:levels, 2:] - wind_terms[levels:, :-2]
    grad_static = static_control + BETA_STATIC * level_sigma[:, None, None] * (
        adjoint[0] + transported
    )
    forcing = factor * jnp.sum(perturbations.astype(jnp.float32) * adjoint[:, None], axis=0)
    smoothed_forcing = smooth(
        forcing.reshape(members * levels, strip_rows, row_length), diffusion_rim
    )
    grad_ens = ens_control + smoothed_forcing.reshape(members, levels, strip_rows, row_length)
    return (grad_ens, grad_static, departures)


def solution(mesh):
    return jax.shard_map(
        per_device,
        mesh=mesh,
        in_specs=(
            P("ens", None, "tile", None),
            P(None, "tile", None),
            P(None, "ens", None, "tile", None),
            P(),
            P("tile", None),
            P("tile", None),
            P("tile", None),
            P("tile"),
            P("tile"),
            P("tile"),
            P("tile"),
            P(None, "tile"),
        ),
        out_specs=(P("ens", None, "tile", None), P(None, "tile", None), P("tile")),
        check_vma=False,
    )
```

profile of v0, /device:TPU:1, one launch (start us, length us, event | category | flops | bytes accessed | tf_op | source)
XLA Modules:
  0.0 440.1 jit_solution(12667603522436705478)
XLA Ops:
  10.9 6.0 %collective-permute-start.8 = (f32[9,4,1024]{2,1,0:T(4,128)}, f32[9,4,1024]{2,1,0:T(4,128)}, u32[]{:S(2)}, u32[]{:S(2)}) collective-permute-start(f32[9,4,1024]{2,1,0:T(4,128)} %pad_maximum_fusion.16), channel_id=1, source_target_pairs={{0,1},{1,2},{2,3},{3,4},{4,5},{5,6},{6,7},{7,8},{8,9},{9,10},{10,1... | collective-permute-start | bytes 442376 | tf_op jit(solution)/shard_map/ppermute | solution.py:24
  23.4 5.1 %collective-permute-start.1 = (f32[64,1,1024]{2,1,0:T(1,128)}, f32[64,1,1024]{2,1,0:T(1,128)}, u32[]{:S(2)}, u32[]{:S(2)}) collective-permute-start(f32[64,1,1024]{2,1,0:T(1,128)} %get-tuple-element.60), channel_id=1, source_target_pairs={{0,1},{1,2},{2,3},{3,4},{4,5},{5,6},{6,7},{7,8},{8,9},{9,10},{10,1... | collective-permute-start | bytes 786440 | tf_op jit(solution)/shard_map/ppermute | solution.py:24
  29.5 23.0 %gather_fusion = s32[4096]{0:T(1024)S(1)} fusion(s32[4096]{0:T(1024)S(1)} %copy-done, s32[4096]{0:T(1024)S(1)} %broadcast_clamp_fusion.1), kind=kCustom, calls=%fused_computation | custom fusion | bytes 49152 | tf_op jit(solution)/shard_map/gather | solution.py:97
  53.2 10.8 %all-to-all-start = ((s32[32,1,128]{2,1,0:T(1,128)}), s32[32,1,128]{2,1,0:T(1,128)S(1)}, u32[]{:S(2)}, u32[]{:S(2)}) async-start(s32[32,1,128]{2,1,0:T(1,128)} %compare_select_fusion), calls=%async_computation | async-start | bytes 32768 | tf_op jit(solution)/shard_map/all_to_all | solution.py:101
  68.8 4.5 %all-to-all-done = s32[32,1,128]{2,1,0:T(1,128)S(1)} async-done(((s32[32,1,128]{2,1,0:T(1,128)}), s32[32,1,128]{2,1,0:T(1,128)S(1)}, u32[]{:S(2)}, u32[]{:S(2)}) %all-to-all-start) | async-done | bytes 16416 | tf_op jit(solution)/shard_map/all_to_all | solution.py:101
  73.9 3.0 broadcast_multiply_fusion.5
  77.4 2.5 collective-permute-start.2
  79.9 4.5 %collective-permute-start.3 = (f32[64,1,1024]{2,1,0:T(1,128)S(1)}, f32[64,1,1024]{2,1,0:T(1,128)S(1)}, u32[]{:S(2)}, u32[]{:S(2)}) collective-permute-start(f32[64,1,1024]{2,1,0:T(1,128)S(1)} %get-tuple-element.54), channel_id=1, source_target_pairs={{0,1},{1,2},{2,3},{3,4},{4,5},{5,6},{6,7},{7,8},{8,9},{9,10},{10,1... | collective-permute-start | bytes 786440 | tf_op jit(solution)/shard_map/ppermute | solution.py:24
  92.0 5.9 %collective-permute-start.5 = (f32[64,1,1024]{2,1,0:T(1,128)S(1)}, f32[64,1,1024]{2,1,0:T(1,128)S(1)}, u32[]{:S(2)}, u32[]{:S(2)}) collective-permute-start(f32[64,1,1024]{2,1,0:T(1,128)S(1)} %get-tuple-element.48), channel_id=1, source_target_pairs={{0,1},{1,2},{2,3},{3,4},{4,5},{5,6},{6,7},{7,8},{8,9},{9,10},{10,1... | collective-permute-start | bytes 786440 | tf_op jit(solution)/shard_map/ppermute | solution.py:24
  105.8 6.1 %collective-permute-start.7 = (f32[64,1,1024]{2,1,0:T(1,128)S(1)}, f32[64,1,1024]{2,1,0:T(1,128)S(1)}, u32[]{:S(2)}, u32[]{:S(2)}) collective-permute-start(f32[64,1,1024]{2,1,0:T(1,128)S(1)} %get-tuple-element.46), channel_id=1, source_target_pairs={{0,1},{1,2},{2,3},{3,4},{4,5},{5,6},{6,7},{7,8},{8,9},{9,10},{10,1... | collective-permute-start | bytes 786440 | tf_op jit(solution)/shard_map/ppermute | solution.py:24
  113.8 2.1 collective-permute-done.7
  120.5 76.2 %all-reduce.2.cloned.1.call-done = f32[2,8,4,1024]{3,2,1,0:T(4,128)} async-done(((f32[2,8,4,1024]{3,2,1,0:T(4,128)}), f32[2,8,4,1024]{3,2,1,0:T(4,128)}) %all-reduce.2.cloned.1.call-update) | async-done | bytes 262160 | tf_op jit(solution)/shard_map/psum | solution.py:89
  197.8 2.6 copy.32
  200.5 12.9 %gather_fusion.3 = f32[4096,8]{1,0:T(8,128)S(1)} fusion(f32[8,8192]{0,1:T(8,128)} %bitcast.73, s32[4096]{0:T(1024)S(1)} %broadcast_clamp_fusion), kind=kCustom, calls=%fused_computation.3 | custom fusion | bytes 278528 | tf_op jit(solution)/shard_map/gather | solution.py:103
  214.6 15.2 %all-to-all-start.1 = ((f32[32,8,128]{2,1,0:T(8,128)}), f32[32,8,128]{2,1,0:T(8,128)S(1)}, u32[]{:S(2)}, u32[]{:S(2)}) async-start(f32[32,8,128]{2,1,0:T(8,128)} %bitcast.15), calls=%async_computation.1 | async-start | bytes 262144 | tf_op jit(solution)/shard_map/all_to_all | solution.py:104
  231.4 14.1 %gather_fusion.1 = f32[4096,8]{1,0:T(8,128)} fusion(f32[8,4096]{0,1:T(8,128)S(1)} %copy.30, s32[4096]{0:T(1024)S(1)} %broadcast_clamp_fusion.1), kind=kCustom, calls=%fused_computation.1 | custom fusion | bytes 278528 | tf_op jit(solution)/shard_map/gather | solution.py:100
  245.5 2.2 copy.31
  247.6 23.0 %gather_fusion.2 = f32[4096]{0:T(1024)S(1)} fusion(f32[4096]{0:T(1024)S(1)} %copy-done.2, s32[4096]{0:T(1024)S(1)} %broadcast_clamp_fusion.1), kind=kCustom, calls=%fused_computation.2 | custom fusion | bytes 49152 | tf_op jit(solution)/shard_map/gather | solution.py:99
  270.7 23.0 %gather_fusion.4 = f32[4096]{0:T(1024)S(1)} fusion(f32[4096]{0:T(1024)S(1)} %copy-done.3, s32[4096]{0:T(1024)S(1)} %broadcast_clamp_fusion.1), kind=kCustom, calls=%fused_computation.4 | custom fusion | bytes 49152 | tf_op jit(solution)/shard_map/gather | solution.py:98
  294.6 9.8 %all-to-all-start.2 = ((f32[32,8,128]{2,1,0:T(8,128)}), f32[32,8,128]{2,1,0:T(8,128)S(1)}, u32[]{:S(2)}, u32[]{:S(2)}) async-start(f32[32,8,128]{2,1,0:T(8,128)} %bitcast_multiply_fusion.3), calls=%async_computation.2 | async-start | bytes 262144 | tf_op jit(solution)/shard_map/all_to_all | solution.py:107
  304.4 29.4 %scatter_custom_fusion.1 = f32[4096]{0:T(1024)} fusion(s32[4096]{0:T(1024)S(1)} %fusion.75, f32[4096]{0:T(1024)S(1)} %get-tuple-element.3, f32[]{:T(128)} %constant.10.clone.1), kind=kCustom, calls=%fused_computation.143 | custom fusion | flops 4096 | bytes 16388 | tf_op jit(solution)/shard_map/scatter-add | solution.py:113
  334.4 28.1 %scatter_custom_fusion = f32[8,8192]{0,1:T(8,128)} fusion(s32[4096]{0:T(1024)} %bitcast.83, f32[4096,8]{1,0:T(8,128)S(1)} %copy.34, f32[]{:T(128)} %constant.10.clone.1), kind=kCustom, calls=%fused_computation.11 | custom fusion | flops 32768 | bytes 262656 | tf_op jit(solution)/shard_map/scatter-add | solution.py:118
  362.5 2.9 copy.35
  369.8 6.2 %collective-permute-start.19 = (f32[16,1,1024]{2,1,0:T(1,128)S(1)}, f32[16,1,1024]{2,1,0:T(1,128)S(1)}, u32[]{:S(2)}, u32[]{:S(2)}) collective-permute-start(f32[16,1,1024]{2,1,0:T(1,128)S(1)} %get-tuple-element.70), channel_id=1, source_target_pairs={{0,1},{1,2},{2,3},{3,4},{4,5},{5,6},{6,7},{7,8},{8,9},{9,10},{10,1... | collective-permute-start | bytes 196616 | tf_op jit(solution)/shard_map/ppermute | solution.py:24
  377.9 5.1 %collective-permute-start.11 = (f32[64,1,1024]{2,1,0:T(1,128)S(1)}, f32[64,1,1024]{2,1,0:T(1,128)S(1)}, u32[]{:S(2)}, u32[]{:S(2)}) collective-permute-start(f32[64,1,1024]{2,1,0:T(1,128)S(1)} %get-tuple-element.36), channel_id=1, source_target_pairs={{0,1},{1,2},{2,3},{3,4},{4,5},{5,6},{6,7},{7,8},{8,9},{9,10},{10,1... | collective-permute-start | bytes 786440 | tf_op jit(solution)/shard_map/ppermute | solution.py:24
  386.8 2.1 broadcast_multiply_fusion.2
  391.3 5.9 %collective-permute-start.13 = (f32[64,1,1024]{2,1,0:T(1,128)S(1)}, f32[64,1,1024]{2,1,0:T(1,128)S(1)}, u32[]{:S(2)}, u32[]{:S(2)}) collective-permute-start(f32[64,1,1024]{2,1,0:T(1,128)S(1)} %get-tuple-element.30), channel_id=1, source_target_pairs={{0,1},{1,2},{2,3},{3,4},{4,5},{5,6},{6,7},{7,8},{8,9},{9,10},{10,1... | collective-permute-start | bytes 786440 | tf_op jit(solution)/shard_map/ppermute | solution.py:24
  399.3 2.1 collective-permute-done.13
  405.6 5.9 %collective-permute-start.15 = (f32[64,1,1024]{2,1,0:T(1,128)S(1)}, f32[64,1,1024]{2,1,0:T(1,128)S(1)}, u32[]{:S(2)}, u32[]{:S(2)}) collective-permute-start(f32[64,1,1024]{2,1,0:T(1,128)S(1)} %get-tuple-element.24), channel_id=1, source_target_pairs={{0,1},{1,2},{2,3},{3,4},{4,5},{5,6},{6,7},{7,8},{8,9},{9,10},{10,1... | collective-permute-start | bytes 786440 | tf_op jit(solution)/shard_map/ppermute | solution.py:24
  413.7 2.1 collective-permute-done.15
  420.0 5.9 %collective-permute-start.17 = (f32[64,1,1024]{2,1,0:T(1,128)S(1)}, f32[64,1,1024]{2,1,0:T(1,128)S(1)}, u32[]{:S(2)}, u32[]{:S(2)}) collective-permute-start(f32[64,1,1024]{2,1,0:T(1,128)S(1)} %get-tuple-element.22), channel_id=1, source_target_pairs={{0,1},{1,2},{2,3},{3,4},{4,5},{5,6},{6,7},{7,8},{8,9},{9,10},{10,1... | collective-permute-start | bytes 786440 | tf_op jit(solution)/shard_map/ppermute | solution.py:24
  428.0 2.1 collective-permute-done.17
  (142 shorter events, 74.7 us)
Async XLA Ops:
  7.2 22.3 %copy-start = (s32[4096]{0:T(1024)S(1)}, s32[4096]{0:T(1024)}, u32[]{:S(2)}) copy-start(s32[4096]{0:T(1024)} %param.19) | copy-start | bytes 49156
  7.2 21.4 %copy-start.19 = (s32[32]{0:T(128)S(1)}, s32[32]{0:T(128)}, u32[]{:S(2)}) copy-start(s32[32]{0:T(128)} %param.20) | copy-start | bytes 388
  9.2 58.2 %copy-start.17 = (f32[8]{0:T(128)}, f32[8]{0:T(128)S(1)}, u32[]{:S(2)}) copy-start(f32[8]{0:T(128)S(1)} %broadcast_multiply_fusion.9) | copy-start | bytes 100
  10.9 108.3 %collective-permute-start.8 = (f32[9,4,1024]{2,1,0:T(4,128)}, f32[9,4,1024]{2,1,0:T(4,128)}, u32[]{:S(2)}, u32[]{:S(2)}) collective-permute-start(f32[9,4,1024]{2,1,0:T(4,128)} %pad_maximum_fusion.16), channel_id=1, source_target_pairs={{0,1},{1,2},{2,3},{3,4},{4,5},{5,6},{6,7},{7,8},{8,9},{9,10},{10,1... | collective-permute-start | bytes 442376 | tf_op jit(solution)/shard_map/ppermute | solution.py:24
  16.9 102.3 %collective-permute-start.9 = (f32[9,4,1024]{2,1,0:T(4,128)}, f32[9,4,1024]{2,1,0:T(4,128)}, u32[]{:S(2)}, u32[]{:S(2)}) collective-permute-start(f32[9,4,1024]{2,1,0:T(4,128)} %pad_maximum_fusion.16), channel_id=1, source_target_pairs={{1,0},{2,1},{3,2},{4,3},{5,4},{6,5},{7,6},{8,7},{9,8},{10,9},{11,1... | collective-permute-start | bytes 442376 | tf_op jit(solution)/shard_map/ppermute | solution.py:25
  21.5 52.4 %collective-permute-start = (f32[64,1,1024]{2,1,0:T(1,128)}, f32[64,1,1024]{2,1,0:T(1,128)}, u32[]{:S(2)}, u32[]{:S(2)}) collective-permute-start(f32[64,1,1024]{2,1,0:T(1,128)} %get-tuple-element.59), channel_id=1, source_target_pairs={{1,0},{2,1},{3,2},{4,3},{5,4},{6,5},{7,6},{8,7},{9,8},{10,9},{11,1... | collective-permute-start | bytes 786440 | tf_op jit(solution)/shard_map/ppermute | solution.py:25
  23.4 50.5 %collective-permute-start.1 = (f32[64,1,1024]{2,1,0:T(1,128)}, f32[64,1,1024]{2,1,0:T(1,128)}, u32[]{:S(2)}, u32[]{:S(2)}) collective-permute-start(f32[64,1,1024]{2,1,0:T(1,128)} %get-tuple-element.60), channel_id=1, source_target_pairs={{0,1},{1,2},{2,3},{3,4},{4,5},{5,6},{6,7},{7,8},{8,9},{9,10},{10,1... | collective-permute-start | bytes 786440 | tf_op jit(solution)/shard_map/ppermute | solution.py:24
  53.2 20.1 %all-to-all-start = ((s32[32,1,128]{2,1,0:T(1,128)}), s32[32,1,128]{2,1,0:T(1,128)S(1)}, u32[]{:S(2)}, u32[]{:S(2)}) async-start(s32[32,1,128]{2,1,0:T(1,128)} %compare_select_fusion), calls=%async_computation | async-start | bytes 32768 | tf_op jit(solution)/shard_map/all_to_all | solution.py:101
  64.1 132.7 %all-reduce.2.cloned.1.call-start = ((), (), s32[]{:S(2)}) async-start(), calls=%async_computation.3 | async-start | bytes 524288 | tf_op jit(solution)/shard_map/psum | solution.py:89
  77.4 9.2 %collective-permute-start.2 = (f32[64,1,1024]{2,1,0:T(1,128)S(1)}, f32[64,1,1024]{2,1,0:T(1,128)S(1)}, u32[]{:S(2)}, u32[]{:S(2)}) collective-permute-start(f32[64,1,1024]{2,1,0:T(1,128)S(1)} %get-tuple-element.53), channel_id=1, source_target_pairs={{1,0},{2,1},{3,2},{4,3},{5,4},{6,5},{7,6},{8,7},{9,8},{10,9},{11,1... | collective-permute-start | bytes 786440 | tf_op jit(solution)/shard_map/ppermute | solution.py:25
  79.9 7.8 %collective-permute-start.3 = (f32[64,1,1024]{2,1,0:T(1,128)S(1)}, f32[64,1,1024]{2,1,0:T(1,128)S(1)}, u32[]{:S(2)}, u32[]{:S(2)}) collective-permute-start(f32[64,1,1024]{2,1,0:T(1,128)S(1)} %get-tuple-element.54), channel_id=1, source_target_pairs={{0,1},{1,2},{2,3},{3,4},{4,5},{5,6},{6,7},{7,8},{8,9},{9,10},{10,1... | collective-permute-start | bytes 786440 | tf_op jit(solution)/shard_map/ppermute | solution.py:24
  90.1 9.9 %collective-permute-start.4 = (f32[64,1,1024]{2,1,0:T(1,128)S(1)}, f32[64,1,1024]{2,1,0:T(1,128)S(1)}, u32[]{:S(2)}, u32[]{:S(2)}) collective-permute-start(f32[64,1,1024]{2,1,0:T(1,128)S(1)} %get-tuple-element.47), channel_id=1, source_target_pairs={{1,0},{2,1},{3,2},{4,3},{5,4},{6,5},{7,6},{8,7},{9,8},{10,9},{11,1... | collective-permute-start | bytes 786440 | tf_op jit(solution)/shard_map/ppermute | solution.py:25
  92.0 9.5 %collective-permute-start.5 = (f32[64,1,1024]{2,1,0:T(1,128)S(1)}, f32[64,1,1024]{2,1,0:T(1,128)S(1)}, u32[]{:S(2)}, u32[]{:S(2)}) collective-permute-start(f32[64,1,1024]{2,1,0:T(1,128)S(1)} %get-tuple-element.48), channel_id=1, source_target_pairs={{0,1},{1,2},{2,3},{3,4},{4,5},{5,6},{6,7},{7,8},{8,9},{9,10},{10,1... | collective-permute-start | bytes 786440 | tf_op jit(solution)/shard_map/ppermute | solution.py:24
  103.8 9.9 %collective-permute-start.6 = (f32[64,1,1024]{2,1,0:T(1,128)S(1)}, f32[64,1,1024]{2,1,0:T(1,128)S(1)}, u32[]{:S(2)}, u32[]{:S(2)}) collective-permute-start(f32[64,1,1024]{2,1,0:T(1,128)S(1)} %get-tuple-element.45), channel_id=1, source_target_pairs={{1,0},{2,1},{3,2},{4,3},{5,4},{6,5},{7,6},{8,7},{9,8},{10,9},{11,1... | collective-permute-start | bytes 786440 | tf_op jit(solution)/shard_map/ppermute | solution.py:25
  105.8 10.1 %collective-permute-start.7 = (f32[64,1,1024]{2,1,0:T(1,128)S(1)}, f32[64,1,1024]{2,1,0:T(1,128)S(1)}, u32[]{:S(2)}, u32[]{:S(2)}) collective-permute-start(f32[64,1,1024]{2,1,0:T(1,128)S(1)} %get-tuple-element.46), channel_id=1, source_target_pairs={{0,1},{1,2},{2,3},{3,4},{4,5},{5,6},{6,7},{7,8},{8,9},{9,10},{10,1... | collective-permute-start | bytes 786440 | tf_op jit(solution)/shard_map/ppermute | solution.py:24
  117.8 79.0 %copy-start.10 = (f32[1,8,4,1024]{3,2,1,0:T(4,128)S(1)}, f32[1,8,4,1024]{3,2,1,0:T(4,128)}, u32[]{:S(2)}) copy-start(f32[1,8,4,1024]{3,2,1,0:T(4,128)} %fusion.114) | copy-start | bytes 393220
  214.6 79.1 %all-to-all-start.1 = ((f32[32,8,128]{2,1,0:T(8,128)}), f32[32,8,128]{2,1,0:T(8,128)S(1)}, u32[]{:S(2)}, u32[]{:S(2)}) async-start(f32[32,8,128]{2,1,0:T(8,128)} %bitcast.15), calls=%async_computation.1 | async-start | bytes 262144 | tf_op jit(solution)/shard_map/all_to_all | solution.py:104
  231.4 16.3 %copy-start.2 = (f32[4096]{0:T(1024)S(1)}, f32[4096]{0:T(1024)}, u32[]{:S(2)}) copy-start(f32[4096]{0:T(1024)} %param.22) | copy-start | bytes 49156
  247.6 23.1 %copy-start.3 = (f32[4096]{0:T(1024)S(1)}, f32[4096]{0:T(1024)}, u32[]{:S(2)}) copy-start(f32[4096]{0:T(1024)} %param.21) | copy-start | bytes 49156
  270.7 23.1 %copy-start.20 = (s32[32]{0:T(128)S(1)}, s32[32]{0:T(128)}, u32[]{:S(2)}) copy-start(s32[32]{0:T(128)} %param.20) | copy-start | bytes 388
  270.7 33.7 %copy-start.22 = (s32[32]{0:T(128)S(1)}, s32[32]{0:T(128)}, u32[]{:S(2)}) copy-start(s32[32]{0:T(128)} %copy-done.21) | copy-start | bytes 388
  294.6 39.2 %all-to-all-start.2 = ((f32[32,8,128]{2,1,0:T(8,128)}), f32[32,8,128]{2,1,0:T(8,128)S(1)}, u32[]{:S(2)}, u32[]{:S(2)}) async-start(f32[32,8,128]{2,1,0:T(8,128)} %bitcast_multiply_fusion.3), calls=%async_computation.2 | async-start | bytes 262144 | tf_op jit(solution)/shard_map/all_to_all | solution.py:107
  367.8 15.6 %collective-permute-start.18 = (f32[16,1,1024]{2,1,0:T(1,128)S(1)}, f32[16,1,1024]{2,1,0:T(1,128)S(1)}, u32[]{:S(2)}, u32[]{:S(2)}) collective-permute-start(f32[16,1,1024]{2,1,0:T(1,128)S(1)} %get-tuple-element.69), channel_id=1, source_target_pairs={{1,0},{2,1},{3,2},{4,3},{5,4},{6,5},{7,6},{8,7},{9,8},{10,9},{11,1... | collective-permute-start | bytes 196616 | tf_op jit(solution)/shard_map/ppermute | solution.py:25
  369.8 13.6 %collective-permute-start.19 = (f32[16,1,1024]{2,1,0:T(1,128)S(1)}, f32[16,1,1024]{2,1,0:T(1,128)S(1)}, u32[]{:S(2)}, u32[]{:S(2)}) collective-permute-start(f32[16,1,1024]{2,1,0:T(1,128)S(1)} %get-tuple-element.70), channel_id=1, source_target_pairs={{0,1},{1,2},{2,3},{3,4},{4,5},{5,6},{6,7},{7,8},{8,9},{9,10},{10,1... | collective-permute-start | bytes 196616 | tf_op jit(solution)/shard_map/ppermute | solution.py:24
  375.9 9.2 %collective-permute-start.10 = (f32[64,1,1024]{2,1,0:T(1,128)S(1)}, f32[64,1,1024]{2,1,0:T(1,128)S(1)}, u32[]{:S(2)}, u32[]{:S(2)}) collective-permute-start(f32[64,1,1024]{2,1,0:T(1,128)S(1)} %get-tuple-element.35), channel_id=1, source_target_pairs={{1,0},{2,1},{3,2},{4,3},{5,4},{6,5},{7,6},{8,7},{9,8},{10,9},{11,1... | collective-permute-start | bytes 786440 | tf_op jit(solution)/shard_map/ppermute | solution.py:25
  377.9 9.0 %collective-permute-start.11 = (f32[64,1,1024]{2,1,0:T(1,128)S(1)}, f32[64,1,1024]{2,1,0:T(1,128)S(1)}, u32[]{:S(2)}, u32[]{:S(2)}) collective-permute-start(f32[64,1,1024]{2,1,0:T(1,128)S(1)} %get-tuple-element.36), channel_id=1, source_target_pairs={{0,1},{1,2},{2,3},{3,4},{4,5},{5,6},{6,7},{7,8},{8,9},{9,10},{10,1... | collective-permute-start | bytes 786440 | tf_op jit(solution)/shard_map/ppermute | solution.py:24
  389.4 9.9 %collective-permute-start.12 = (f32[64,1,1024]{2,1,0:T(1,128)S(1)}, f32[64,1,1024]{2,1,0:T(1,128)S(1)}, u32[]{:S(2)}, u32[]{:S(2)}) collective-permute-start(f32[64,1,1024]{2,1,0:T(1,128)S(1)} %get-tuple-element.29), channel_id=1, source_target_pairs={{1,0},{2,1},{3,2},{4,3},{5,4},{6,5},{7,6},{8,7},{9,8},{10,9},{11,1... | collective-permute-start | bytes 786440 | tf_op jit(solution)/shard_map/ppermute | solution.py:25
  391.3 10.1 %collective-permute-start.13 = (f32[64,1,1024]{2,1,0:T(1,128)S(1)}, f32[64,1,1024]{2,1,0:T(1,128)S(1)}, u32[]{:S(2)}, u32[]{:S(2)}) collective-permute-start(f32[64,1,1024]{2,1,0:T(1,128)S(1)} %get-tuple-element.30), channel_id=1, source_target_pairs={{0,1},{1,2},{2,3},{3,4},{4,5},{5,6},{6,7},{7,8},{8,9},{9,10},{10,1... | collective-permute-start | bytes 786440 | tf_op jit(solution)/shard_map/ppermute | solution.py:24
  403.7 9.9 %collective-permute-start.14 = (f32[64,1,1024]{2,1,0:T(1,128)S(1)}, f32[64,1,1024]{2,1,0:T(1,128)S(1)}, u32[]{:S(2)}, u32[]{:S(2)}) collective-permute-start(f32[64,1,1024]{2,1,0:T(1,128)S(1)} %get-tuple-element.23), channel_id=1, source_target_pairs={{1,0},{2,1},{3,2},{4,3},{5,4},{6,5},{7,6},{8,7},{9,8},{10,9},{11,1... | collective-permute-start | bytes 786440 | tf_op jit(solution)/shard_map/ppermute | solution.py:25
  405.6 10.1 %collective-permute-start.15 = (f32[64,1,1024]{2,1,0:T(1,128)S(1)}, f32[64,1,1024]{2,1,0:T(1,128)S(1)}, u32[]{:S(2)}, u32[]{:S(2)}) collective-permute-start(f32[64,1,1024]{2,1,0:T(1,128)S(1)} %get-tuple-element.24), channel_id=1, source_target_pairs={{0,1},{1,2},{2,3},{3,4},{4,5},{5,6},{6,7},{7,8},{8,9},{9,10},{10,1... | collective-permute-start | bytes 786440 | tf_op jit(solution)/shard_map/ppermute | solution.py:24
  418.1 9.9 %collective-permute-start.16 = (f32[64,1,1024]{2,1,0:T(1,128)S(1)}, f32[64,1,1024]{2,1,0:T(1,128)S(1)}, u32[]{:S(2)}, u32[]{:S(2)}) collective-permute-start(f32[64,1,1024]{2,1,0:T(1,128)S(1)} %get-tuple-element.21), channel_id=1, source_target_pairs={{1,0},{2,1},{3,2},{4,3},{5,4},{6,5},{7,6},{8,7},{9,8},{10,9},{11,1... | collective-permute-start | bytes 786440 | tf_op jit(solution)/shard_map/ppermute | solution.py:25
  420.0 10.1 %collective-permute-start.17 = (f32[64,1,1024]{2,1,0:T(1,128)S(1)}, f32[64,1,1024]{2,1,0:T(1,128)S(1)}, u32[]{:S(2)}, u32[]{:S(2)}) collective-permute-start(f32[64,1,1024]{2,1,0:T(1,128)S(1)} %get-tuple-element.22), channel_id=1, source_target_pairs={{0,1},{1,2},{2,3},{3,4},{4,5},{5,6},{6,7},{7,8},{8,9},{9,10},{10,1... | collective-permute-start | bytes 786440 | tf_op jit(solution)/shard_map/ppermute | solution.py:24
  (15 other events, 54.5 us)
Sparse Core Ops, SparseCore 0:
  119.3 77.3 all-reduce.1
where the time goes:
time: 447 us; the launch traced here: 440 us
  local copies, waits for them, and re-layouts  122 us (27%)
  starting transfers between devices  112 us (25%)
  waiting for transfers between devices  102 us (23%)
  other arithmetic  89.4 us (20%)
  between operations  14.9 us (3%)
    psum x1, waiting for transfers between devices, per_device(): lax.psum(partial_sum, 'ens') + jnp.stack([static_first, static_second])  76.2 us
    ppermute x10, starting transfers between devices, padded(): before = lax.ppermute(last, axis, up)  56.7 us
    scatter-add x1, other arithmetic, per_device(): departures = jnp.zeros(obs_column.shape, jnp.float32).at[source].add(jnp....  29.4 us
    scatter-add x1, other arithmetic, per_device(): adjoint = jnp.zeros(columns.shape, jnp.float32).at[:, owned_index].add(jn...  28.1 us
    gather x1, local copies, waits for them, and re-layouts, per_device(): weight_blocks = jnp.where(usable, obs_weight[source], 0.0)  23 us
    gather x1, local copies, waits for them, and re-layouts, per_device(): column_blocks = jnp.where(usable, obs_column[source], -1)  23 us
    gather x1, local copies, waits for them, and re-layouts, per_device(): value_blocks = obs_value[source]  23 us
    ppermute x10, starting transfers between devices, padded(): after = lax.ppermute(leading, axis, down)  19.8 us
  transfers between devices with their start and end apart: 24, of which 16 were waited for; matrix products, arithmetic and copies ran while one was open for 33% of the time, Pallas kernels for 0%

commit v1 on v0

v1 whole, which is shorter than its diff:
```python
import functools
import math

import jax
import jax.numpy as jnp
from jax import lax
from jax.experimental import pallas as pl
from jax.experimental.pallas import tpu as pltpu
from jax.sharding import PartitionSpec as P

NT = 2
NDIFF = 4
BETA_ENS = 0.8
BETA_STATIC = 0.6
DIFF_BASE = 0.06
LANES = 128
MESH = pl.DeviceIdType.MESH
F32 = jnp.float32
BF16 = jnp.bfloat16


def split3(x):
    a = x.astype(BF16)
    rest = x - a.astype(F32)
    b = rest.astype(BF16)
    c = (rest - b.astype(F32)).astype(BF16)
    return a, b, c


def left(x):
    return pltpu.roll(x, 1, 1)


def right(x):
    return pltpu.roll(x, x.shape[1] - 1, 1)


def kernel(
    factor,
    ens,
    tiles,
    ctl,
    stc,
    per,
    sigma,
    cls,
    east,
    north,
    ocol,
    ocnt,
    oval,
    owgt,
    oker,
    gens,
    gsta,
    gdep,
    okb,
    dif,
    dif_u,
    dif_d,
    dbc,
    dsq,
    fin,
    sta,
    sta_u,
    sta_d,
    stb,
    wnd_u,
    wnd_d,
    rcv_wu,
    rcv_wd,
    cc,
    cu,
    cd,
    pp,
    ff,
    fu,
    fd,
    wa,
    wb,
    acc,
    accb,
    rbuf,
    obs_s,
    obs_r,
    onehot,
    himask,
    adjb,
    abuf,
    adjf,
    depp,
    dbuf,
    deps,
    depr,
    s_pre,
    r_pre,
    s_c,
    r_c,
    s_f,
    r_f,
    s_obs,
    r_obs,
    s_rs,
    r_rs,
    s_ag,
    r_ag,
    s_dg,
    r_dg,
    s_w,
    r_w,
    s_dep,
    r_dep,
):
    members, lev, rows, width = ctl.shape
    hi_n = NT * rows
    e = lax.axis_index("ens")
    t = lax.axis_index("tile")
    up = lax.rem(t + tiles - 1, tiles)
    down = lax.rem(t + 1, tiles)
    first = t == 0
    last = t == tiles - 1

    def remote(src, dst, ssem, rsem, e_to, t_to):
        return pltpu.make_async_remote_copy(
            src_ref=src,
            dst_ref=dst,
            send_sem=ssem,
            recv_sem=rsem,
            device_id=(e_to, t_to),
            device_id_type=MESH,
        )

    def loop(n, body):
        def step(i, carry):
            body(i)
            return carry

        lax.fori_loop(0, n, step, 0)

    def peer_e(k):
        return lax.rem(e + k, ens)

    def peer_t(k):
        return lax.rem(t + k, tiles)

    barrier = pltpu.get_barrier_semaphore()
    loop(
        tiles - 1,
        lambda k: pl.semaphore_signal(
            barrier, inc=1, device_id=(e, peer_t(k + 1)), device_id_type=MESH
        ),
    )
    loop(
        ens - 1,
        lambda k: pl.semaphore_signal(
            barrier, inc=1, device_id=(peer_e(k + 1), t), device_id_type=MESH
        ),
    )
    dif[...] = jnp.sqrt(DIFF_BASE * (cls[...].astype(F32) + 1.0))
    sub = lax.broadcasted_iota(jnp.int32, (lev, width), 0)
    scale = jnp.zeros((lev, width), F32)
    for l in range(lev):
        scale = jnp.where(sub == l, BETA_STATIC * sigma[l], scale)
    for r in range(rows):
        sta[r] = scale * stc[:, r, :]
    pl.semaphore_wait(barrier, tiles - 1 + ens - 1)

    pre = [
        remote(dif, dif_u, s_pre.at[0], r_pre.at[0], e, down),
        remote(dif, dif_d, s_pre.at[1], r_pre.at[1], e, up),
        remote(sta.at[rows - 1], sta_u, s_pre.at[2], r_pre.at[2], e, down),
        remote(sta.at[0], sta_d, s_pre.at[3], r_pre.at[3], e, up),
    ]
    for copy in pre:
        copy.start()

    def halo(m, own, from_up, from_down, ssem, rsem):
        return (
            remote(own.at[m], from_up.at[m], ssem.at[0, m], rsem.at[0, m], e, down),
            remote(own.at[m], from_down.at[m], ssem.at[1, m], rsem.at[1, m], e, up),
        )

    def send_control(m):
        for r in range(rows):
            cc[m, r] = ctl[m, :, r, :]
        for copy in halo(m, cc, cu, cd, s_c, r_c):
            copy.start()

    loop(members, send_control)

    count = jnp.broadcast_to(ocnt[...].astype(F32), (tiles, tiles))
    d_sub = lax.broadcasted_iota(jnp.int32, (tiles, tiles), 0)
    d_lane = lax.broadcasted_iota(jnp.int32, (tiles, tiles), 1)
    count_col = jnp.sum(
        jnp.where(d_lane == d_sub, count, 0.0), axis=1, keepdims=True
    )
    start_col = jnp.sum(jnp.where(d_lane < d_sub, count, 0.0), axis=1, keepdims=True)
    start_row = jnp.sum(
        jnp.where(d_sub < d_lane, jnp.broadcast_to(count_col, (tiles, tiles)), 0.0),
        axis=0,
        keepdims=True,
    )
    begin = jnp.broadcast_to(start_col, (tiles, LANES)).astype(jnp.int32)
    shift = begin & (LANES - 1)
    lane = lax.broadcasted_iota(jnp.int32, (tiles, LANES), 1)
    usable = lane < jnp.broadcast_to(count_col, (tiles, LANES)).astype(jnp.int32)

    def turn(x, back):
        for bit in range(LANES.bit_length() - 1):
            by = LANES - (1 << bit) if back else 1 << bit
            x = jnp.where(shift & (1 << bit) != 0, pltpu.roll(x, by, 1), x)
        return x

    line_col = jnp.broadcast_to(start_col, (tiles, tiles)).astype(jnp.int32) // LANES
    pick = jnp.concatenate(
        [jnp.where(d_lane == line_col, 1.0, 0.0), jnp.where(d_lane == line_col + 1, 1.0, 0.0)],
        axis=0,
    ).astype(BF16)
    for b in range(tiles):
        okb[b] = oker[:, b * LANES : (b + 1) * LANES]
    for q in range(lev + 3):
        if q < lev:
            part = okb[:, q, :]
        else:
            part = (ocol, oval, owgt)[q - lev][...].astype(F32)
        two = sum(
            jnp.dot(pick, piece, preferred_element_type=F32) for piece in split3(part)
        )
        value = turn(jnp.where(lane >= shift, two[0:tiles], two[tiles : 2 * tiles]), True)
        if q == lev:
            value = jnp.where(usable, value, -1.0)
        obs_s[:, q, :] = value
    for q in range(lev + 3, 2 * lev):
        obs_s[:, q, :] = jnp.zeros((tiles, LANES), F32)

    def obs_copy(k):
        d = peer_t(k)
        return remote(obs_s.at[d], obs_r.at[t], s_obs.at[d], r_obs.at[t], e, d)

    loop(tiles - 1, lambda k: obs_copy(k + 1).start())
    obs_r[t] = obs_s[t]

    def spread(m):
        for s in range(NT):
            block = per[s, m].astype(F32)
            for r in range(rows):
                pp[s, m, r] = block[:, r, :]

    loop(members, spread)

    pre[0].wait_recv()
    pre[1].wait_recv()
    above = jnp.where(first, 0.0, dif_u[...])
    below = jnp.where(last, 0.0, dif_d[...])
    own = dif[...]
    total_rows = rows + 2 * NDIFF
    for i in range(total_rows):
        src = above if i < NDIFF else (own if i < NDIFF + rows else below)
        j = i if i < NDIFF else (i - NDIFF if i < NDIFF + rows else i - NDIFF - rows)
        line = jnp.broadcast_to(src[j : j + 1, :], (lev, width))
        dbc[i] = line
        dsq[i] = line * line
        if NDIFF <= i < NDIFF + rows:
            fin[i - NDIFF] = factor / line

    pre[2].wait_recv()
    pre[3].wait_recv()

    def winds(r):
        we = jnp.broadcast_to(east[r : r + 1, :], (lev, width))
        wn = jnp.broadcast_to(north[r : r + 1, :], (lev, width))
        return (
            jnp.maximum(we, 0.0),
            jnp.minimum(we, 0.0),
            jnp.maximum(wn, 0.0),
            jnp.minimum(wn, 0.0),
        )

    for r in range(rows):
        ep, em, np_, nm = winds(r)
        q = sta[r]
        above = sta[r - 1] if r else jnp.where(first, 0.0, sta_u[...])
        below = sta[r + 1] if r < rows - 1 else jnp.where(last, 0.0, sta_d[...])
        moved = q - ep * (q - left(q)) - em * (right(q) - q)
        moved = moved - np_ * (q - above) - nm * (below - q)
        for b in range(ens):
            stb[b, r] = q[:, b * LANES : (b + 1) * LANES]
            stb[b, rows + r] = moved[:, b * LANES : (b + 1) * LANES]

    def obs_wait(k):
        s = peer_t(k + 1)
        remote(obs_s.at[s], obs_r.at[s], s_obs.at[s], r_obs.at[s], e, s).wait_recv()

    loop(tiles - 1, obs_wait)
    pairs = tiles // 2

    def lines_of(g, i):
        return jnp.concatenate(
            [obs_r[2 * g, i : i + 1, :], obs_r[2 * g + 1, i : i + 1, :]], axis=1
        )

    lo_iota = lax.broadcasted_iota(jnp.int32, (LANES, 2 * LANES), 0)

    def hot(g):
        col = lines_of(g, lev).astype(jnp.int32)
        lo = col & (LANES - 1)
        block = (col // LANES) & (ens - 1)
        hi = col // width
        hi = jnp.where((col >= 0) & (block == e), hi, -1)
        himask[g] = jnp.broadcast_to(hi, (lev, 2 * LANES))
        onehot[g] = jnp.where(
            jnp.broadcast_to(lo, (LANES, 2 * LANES)) == lo_iota, 1.0, 0.0
        ).astype(BF16)

    loop(pairs, hot)

    def smooth(m, center, from_up, from_down):
        for i in range(total_rows):
            if i < NDIFF:
                line = from_up[m, i]
            elif i < NDIFF + rows:
                line = center[m, i - NDIFF]
            else:
                line = from_down[m, i - NDIFF - rows]
            wa[i] = dbc[i] * line
        src, dst = wa, wb
        for step in range(NDIFF):
            for i in range(step + 1, total_rows - 1 - step):
                w = src[i]
                lap = src[i + 1] + src[i - 1] + left(w) + right(w) - 4.0 * w
                dst[i] = w + dsq[i] * lap
            src, dst = dst, src
        return src

    for h in range(hi_n):
        acc[h] = jnp.zeros((lev, width), F32)

    def forward(m):
        for copy in halo(m, cc, cu, cd, s_c, r_c):
            copy.wait_recv()
        res = smooth(m, cc, cu, cd)
        for r in range(rows):
            w = res[NDIFF + r]
            for s in range(NT):
                acc[s * rows + r] += pp[s, m, r] * w

    loop(members, forward)

    for h in range(hi_n):
        value = acc[h] * fin[h % rows]
        for b in range(ens):
            accb[b, h] = value[:, b * LANES : (b + 1) * LANES]

    def rs_copy(k):
        to = peer_e(k)
        return remote(accb.at[to], rbuf.at[e], s_rs.at[to], r_rs.at[e], to, t)

    loop(ens - 1, lambda k: rs_copy(k + 1).start())

    def rs_wait(k):
        s = peer_e(k + 1)
        remote(accb.at[s], rbuf.at[s], s_rs.at[s], r_rs.at[s], s, t).wait_recv()

    loop(ens - 1, rs_wait)
    rbuf[e] = accb[e]
    parts = ([], [], [])
    for h in range(hi_n):
        value = stb[e, h]
        for b in range(ens):
            value = value + rbuf[b, h]
        for store, piece in zip(parts, split3(value)):
            store.append(piece)
    table = jnp.concatenate(parts[0] + parts[1] + parts[2], axis=0)
    points = hi_n * lev

    def observe(g, total):
        flat = jnp.dot(table, onehot[g], preferred_element_type=F32)
        flat = flat[0:points] + flat[points : 2 * points] + flat[2 * points : 3 * points]
        hi = himask[g]
        kern = jnp.concatenate(
            [obs_r[2 * g, 0:lev, :], obs_r[2 * g + 1, 0:lev, :]], axis=1
        )
        profile = jnp.zeros((lev, 2 * LANES), F32)
        for h in range(hi_n):
            profile = jnp.where(hi == h, flat[h * lev : (h + 1) * lev], profile)
        evolved = jnp.sum(kern * profile, axis=0, keepdims=True)
        dep = lines_of(g, lev + 2) * (evolved - lines_of(g, lev + 1))
        dep = jnp.where(hi[0:1] >= 0, dep, 0.0)
        depp[2 * g] = dep[:, 0:LANES]
        depp[2 * g + 1] = dep[:, LANES : 2 * LANES]
        push = kern * dep
        place = jnp.concatenate(
            [jnp.where(hi == h, push, 0.0) for h in range(hi_n)], axis=0
        )
        return total + lax.dot_general(
            jnp.concatenate(split3(place), axis=0),
            onehot[g],
            (((1,), (1,)), ((), ())),
            preferred_element_type=F32,
        )

    total = lax.fori_loop(0, pairs, observe, jnp.zeros((3 * points, LANES), F32))
    total = total[0:points] + total[points : 2 * points] + total[2 * points : 3 * points]
    for h in range(hi_n):
        adjb[h] = total[h * lev : (h + 1) * lev]

    def ag_copy(k):
        to = peer_e(k)
        return remote(adjb, abuf.at[e], s_ag.at[to], r_ag.at[e], to, t)

    def dg_copy(k):
        to = peer_e(k)
        return remote(depp, dbuf.at[e], s_dg.at[to], r_dg.at[e], to, t)

    loop(ens - 1, lambda k: ag_copy(k + 1).start())
    loop(ens - 1, lambda k: dg_copy(k + 1).start())
    abuf[e] = adjb[...]

    def ag_wait(k):
        s = peer_e(k + 1)
        remote(adjb, abuf.at[s], s_ag.at[s], r_ag.at[s], s, t).wait_recv()

    loop(ens - 1, ag_wait)
    for h in range(hi_n):
        adjf[h] = jnp.concatenate([abuf[b, h] for b in range(ens)], axis=1)

    def force(m):
        for r in range(rows):
            ff[m, r] = pp[0, m, r] * adjf[r] + pp[1, m, r] * adjf[rows + r]
        for copy in halo(m, ff, fu, fd, s_f, r_f):
            copy.start()

    loop(members, force)

    wnd_u[...] = winds(0)[2] * adjf[rows]
    wnd_d[...] = winds(rows - 1)[3] * adjf[2 * rows - 1]
    wind = [
        remote(wnd_d, rcv_wu, s_w.at[0], r_w.at[0], e, down),
        remote(wnd_u, rcv_wd, s_w.at[1], r_w.at[1], e, up),
    ]
    for copy in wind:
        copy.start()

    def dg_wait(k):
        s = peer_e(k + 1)
        remote(depp, dbuf.at[s], s_dg.at[s], r_dg.at[s], s, t).wait_recv()

    loop(ens - 1, dg_wait)
    dbuf[e] = depp[...]

    def gather_dep(s):
        value = dbuf[0, s]
        for b in range(1, ens):
            value = value + dbuf[b, s]
        deps[s] = value

    loop(tiles, gather_dep)

    def dep_copy(k):
        s = peer_t(k)
        return remote(deps.at[s], depr.at[t], s_dep.at[s], r_dep.at[t], e, s)

    loop(tiles - 1, lambda k: dep_copy(k + 1).start())
    depr[t] = deps[t]

    def backward(m):
        for copy in halo(m, ff, fu, fd, s_f, r_f):
            copy.wait_recv()
        res = smooth(m, ff, fu, fd)
        for r in range(rows):
            gens[m, :, r, :] = cc[m, r] + res[NDIFF + r] * fin[r]

    loop(members, backward)

    for copy in wind:
        copy.wait_recv()
    for r in range(rows):
        ep, em, np_, nm = winds(r)
        a = adjf[rows + r]
        if r < rows - 1:
            lower = winds(r + 1)[2] * adjf[rows + r + 1]
        else:
            lower = jnp.where(last, 0.0, rcv_wd[...])
        if r:
            upper = winds(r - 1)[3] * adjf[rows + r - 1]
        else:
            upper = jnp.where(first, 0.0, rcv_wu[...])
        moved = a * (1.0 - ep + em - np_ + nm) + right(ep * a) - left(em * a)
        moved = moved + lower - upper
        gsta[:, r, :] = stc[:, r, :] + scale * (adjf[r] + moved)

    def dep_wait(k):
        s = peer_t(k + 1)
        remote(deps.at[s], depr.at[s], s_dep.at[s], r_dep.at[s], e, s).wait_recv()

    loop(tiles - 1, dep_wait)
    line_row = jnp.broadcast_to(start_row, (tiles, tiles)).astype(jnp.int32) // LANES
    spread0 = jnp.where(d_sub == line_row, 1.0, 0.0).astype(BF16)
    spread1 = jnp.where(d_sub == line_row + 1, 1.0, 0.0).astype(BF16)
    value = turn(jnp.where(usable, depr[:, 0, :], 0.0), False)
    out = jnp.zeros((tiles, LANES), F32)
    for piece in split3(jnp.where(lane >= shift, value, 0.0)):
        out = out + jnp.dot(spread0, piece, preferred_element_type=F32)
    for piece in split3(jnp.where(lane < shift, value, 0.0)):
        out = out + jnp.dot(spread1, piece, preferred_element_type=F32)
    gdep[...] = out

    for copy in pre + wind:
        copy.wait_send()

    def sent(m):
        for copy in halo(m, cc, cu, cd, s_c, r_c) + halo(m, ff, fu, fd, s_f, r_f):
            copy.wait_send()

    loop(members, sent)

    def sent_t(k):
        obs_copy(k + 1).wait_send()
        dep_copy(k + 1).wait_send()

    loop(tiles - 1, sent_t)

    def sent_e(k):
        rs_copy(k + 1).wait_send()
        ag_copy(k + 1).wait_send()
        dg_copy(k + 1).wait_send()

    loop(ens - 1, sent_e)


def per_device(
    ens_control,
    static_control,
    perturbations,
    level_sigma,
    length_class,
    courant_east,
    courant_north,
    obs_column,
    obs_count,
    obs_value,
    obs_weight,
    obs_kernel,
):
    members, lev, rows, width = ens_control.shape
    ens = lax.axis_size("ens")
    tiles = lax.axis_size("tile")
    factor = BETA_ENS / math.sqrt(ens * members - 1)
    hi_n = NT * rows
    vmem = lambda *shape, dtype=F32: pltpu.VMEM(shape, dtype)
    dma = lambda *shape: pltpu.SemaphoreType.DMA(shape)
    line = (lev, width)
    total_rows = rows + 2 * NDIFF
    fields = (members, rows) + line
    scratch = [
        vmem(tiles, lev, LANES),
        vmem(rows, width),
        vmem(rows, width),
        vmem(rows, width),
        vmem(total_rows, *line),
        vmem(total_rows, *line),
        vmem(rows, *line),
        vmem(rows, *line),
        vmem(*line),
        vmem(*line),
        vmem(ens, hi_n, lev, LANES),
        vmem(*line),
        vmem(*line),
        vmem(*line),
        vmem(*line),
        vmem(*fields),
        vmem(*fields),
        vmem(*fields),
        vmem(NT, *fields),
        vmem(*fields),
        vmem(*fields),
        vmem(*fields),
        vmem(total_rows, *line),
        vmem(total_rows, *line),
        vmem(hi_n, *line),
        vmem(ens, hi_n, lev, LANES),
        vmem(ens, hi_n, lev, LANES),
        vmem(tiles, 2 * lev, LANES),
        vmem(tiles, 2 * lev, LANES),
        vmem(tiles // 2, LANES, 2 * LANES, dtype=BF16),
        vmem(tiles // 2, lev, 2 * LANES, dtype=jnp.int32),
        vmem(hi_n, lev, LANES),
        vmem(ens, hi_n, lev, LANES),
        vmem(hi_n, *line),
        vmem(tiles, 1, LANES),
        vmem(ens, tiles, 1, LANES),
        vmem(tiles, 1, LANES),
        vmem(tiles, 1, LANES),
        dma(4), dma(4),
        dma(2, members), dma(2, members),
        dma(2, members), dma(2, members),
        dma(tiles), dma(tiles),
        dma(ens), dma(ens),
        dma(ens), dma(ens),
        dma(ens), dma(ens),
        dma(2), dma(2),
        dma(tiles), dma(tiles),
    ]
    v = pl.BlockSpec(memory_space=pltpu.VMEM)
    s = pl.BlockSpec(memory_space=pltpu.SMEM)
    shape = jax.ShapeDtypeStruct
    grad_ens, grad_static, departures = pl.pallas_call(
        functools.partial(kernel, factor, ens, tiles),
        out_shape=(
            shape(ens_control.shape, F32),
            shape(static_control.shape, F32),
            shape((tiles, LANES), F32),
        ),
        in_specs=[v, v, v, s, v, v, v, v, v, v, v, v],
        out_specs=(v, v, v),
        scratch_shapes=scratch,
        name="gradient",
        compiler_params=pltpu.CompilerParams(
            collective_id=0, has_side_effects=True, vmem_limit_bytes=56 * 2**20
        ),
    )(
        ens_control,
        static_control,
        perturbations,
        level_sigma,
        length_class,
        courant_east,
        courant_north,
        obs_column.reshape(tiles, LANES),
        obs_count.reshape(1, tiles),
        obs_value.reshape(tiles, LANES),
        obs_weight.reshape(tiles, LANES),
        obs_kernel,
    )
    return (grad_ens, grad_static, departures.reshape(-1))


def solution(mesh):
    return jax.shard_map(
        per_device,
        mesh=mesh,
        in_specs=(
            P("ens", None, "tile", None),
            P(None, "tile", None),
            P(None, "ens", None, "tile", None),
            P(),
            P("tile", None),
            P("tile", None),
            P("tile", None),
            P("tile"),
            P("tile"),
            P("tile"),
            P("tile"),
            P(None, "tile"),
        ),
        out_specs=(P("ens", None, "tile", None), P(None, "tile", None), P("tile")),
        check_vma=False,
    )
```

time: 447 us -> 98.5 us (0.22); the launches traced: 440 us -> 98.3 us
  local copies, waits for them, and re-layouts: 122 us -> 3.63 us
  starting transfers between devices: 112 us -> 0 us
  waiting for transfers between devices: 102 us -> 0 us
  Pallas kernels: 0 us -> 94 us
  other arithmetic: 89.4 us -> 0 us
  between operations: 14.9 us -> 0.65 us
    gather x7 -> x0, local copies, waits for them, and re-layouts: 99.5 us -> none  [the longest x1 23 us: per_device(): weight_blocks = jnp.where(usable, obs_weight[source], 0.0)]
    pallas_call x0 -> x1, Pallas kernels: none -> 94 us  [per_device(): pl.pallas_call(functools.partial(kernel, factor, ens, tiles), out_shape=(...]
    ppermute x20 -> x0, starting transfers between devices: 76.5 us -> none  [the longest x10 56.7 us: padded(): before = lax.ppermute(last, axis, up)]
    psum x1 -> x0, waiting for transfers between devices: 76.2 us -> none  [per_device(): lax.psum(partial_sum, 'ens') + jnp.stack([static_first, static_second])]
    scatter-add x2 -> x0, other arithmetic: 57.5 us -> none  [the longest x1 29.4 us: per_device(): departures = jnp.zeros(obs_column.shape, jnp.float32).at[source].add(jnp....]
    all_to_all x3 -> x0, starting transfers between devices: 35.8 us -> none  [the longest x1 15.2 us: per_device(): lax.all_to_all(owned_profile, 'tile', split_axis=0, concat_axis=0, tiled=...]
    ppermute x20 -> x0, waiting for transfers between devices: 21.2 us -> none  [the longest x10 12.7 us: padded(): before = lax.ppermute(last, axis, up)]
    mul x14 -> x0, other arithmetic: 19.1 us -> none  [the longest x9 15.8 us: smooth(): weighted = padded(stiffness * fields, (('tile', 1),), 1)]
  transfers between devices with their start and end apart: 24 -> 0, of which waited for: 16 -> 0; matrix products, arithmetic and copies ran while one was open for 33% -> 0% of each run, Pallas kernels for 0% -> 0%
where the time goes in v1:
time: 98.5 us; the launch traced here: 98.3 us
  Pallas kernels  94 us (95%)
  local copies, waits for them, and re-layouts  3.63 us (4%)
    pallas_call x1, Pallas kernels, per_device(): pl.pallas_call(functools.partial(kernel, factor, ens, tiles), out_shape=(...  94 us
    unnamed x7, local copies, waits for them, and re-layouts  3.63 us

profile of v1, /device:TPU:1, one launch (start us, length us, event | category | flops | bytes accessed | tf_op | source)
XLA Modules:
  0.0 98.3 jit_solution(9453673200036715976)
XLA Ops:
  0.6 94.0 %gradient.1 = (f32[8,8,4,1024]{3,2,1,0:T(4,128)}, f32[8,4,1024]{2,1,0:T(4,128)}, f32[32,128]{1,0:T(8,128)}) custom-call(f32[8,8,4,1024]{3,2,1,0:T(4,128)} %ctl.1, f32[8,4,1024]{2,1,0:T(4,128)} %stc.1, bf16[2,8,8,4,1024]{4,3,2,1,0:T(4,128)(2,1)} %per.1, f32[8]{0:T(128)} %sigma.1, s32[4,1024]{1,0:T(4,128)} %cls.1, f32[4,1024]{1,0:T(4,128)} %east.1, ...), custom_call_target="tpu_custom_call" | custom-call | tf_op jit(solution)/shard_map/gradient/pallas_call | solution.py:607
  94.7 0.0 copy-start
  94.7 2.3 %copy.18 = f32[8,8,4,1024]{3,2,1,0:T(4,128)} copy(f32[8,8,4,1024]{3,2,1,0:T(4,128)} %get-tuple-element.12) | data formatting | bytes 2097152
  97.0 0.0 copy-done
  97.0 0.0 copy-start.1
  97.0 0.7 copy.19
  97.6 0.1 copy-done.1
  97.7 0.6 copy.20
Async XLA Ops:
  94.7 2.3 %copy-start = (f32[8,4,1024]{2,1,0:T(4,128)S(1)}, f32[8,4,1024]{2,1,0:T(4,128)}, u32[]{:S(2)}) copy-start(f32[8,4,1024]{2,1,0:T(4,128)} %get-tuple-element.13) | copy-start | bytes 393220
  97.0 0.7 copy-start.1

commit v2 on v1

--- a/solution.py
+++ b/solution.py
@@ -39,9 +39,9 @@
     factor,
     ens,
     tiles,
-    ctl,
+    ctl_hbm,
     stc,
-    per,
+    per_hbm,
     sigma,
     cls,
     east,
@@ -51,9 +51,14 @@
     oval,
     owgt,
     oker,
-    gens,
+    gens_hbm,
     gsta,
     gdep,
+    ctl,
+    per,
+    gens,
+    s_in,
+    s_out,
     okb,
     dif,
     dif_u,
@@ -112,6 +117,10 @@
     r_dep,
 ):
     members, lev, rows, width = ctl.shape
+    load_ctl = pltpu.make_async_copy(ctl_hbm, ctl, s_in.at[0])
+    load_per = pltpu.make_async_copy(per_hbm, per, s_in.at[1])
+    load_ctl.start()
+    load_per.start()
     hi_n = NT * rows
     e = lax.axis_index("ens")
     t = lax.axis_index("tile")
@@ -163,6 +172,7 @@
         scale = jnp.where(sub == l, BETA_STATIC * sigma[l], scale)
     for r in range(rows):
         sta[r] = scale * stc[:, r, :]
+    load_ctl.wait()
     pl.semaphore_wait(barrier, tiles - 1 + ens - 1)
 
     pre = [
@@ -186,7 +196,10 @@
         for copy in halo(m, cc, cu, cd, s_c, r_c):
             copy.start()
 
-    loop(members, send_control)
+    def control_part(low, high):
+        lax.fori_loop(low, high, lambda m, c: (send_control(m), c)[1], 0)
+
+    control_part(0, members // 2)
 
     count = jnp.broadcast_to(ocnt[...].astype(F32), (tiles, tiles))
     d_sub = lax.broadcasted_iota(jnp.int32, (tiles, tiles), 0)
@@ -238,6 +251,7 @@
         return remote(obs_s.at[d], obs_r.at[t], s_obs.at[d], r_obs.at[t], e, d)
 
     loop(tiles - 1, lambda k: obs_copy(k + 1).start())
+    control_part(members // 2, members)
     obs_r[t] = obs_s[t]
 
     def spread(m):
@@ -246,6 +260,7 @@
             for r in range(rows):
                 pp[s, m, r] = block[:, r, :]
 
+    load_per.wait()
     loop(members, spread)
 
     pre[0].wait_recv()
@@ -286,33 +301,6 @@
         for b in range(ens):
             stb[b, r] = q[:, b * LANES : (b + 1) * LANES]
             stb[b, rows + r] = moved[:, b * LANES : (b + 1) * LANES]
-
-    def obs_wait(k):
-        s = peer_t(k + 1)
-        remote(obs_s.at[s], obs_r.at[s], s_obs.at[s], r_obs.at[s], e, s).wait_recv()
-
-    loop(tiles - 1, obs_wait)
-    pairs = tiles // 2
-
-    def lines_of(g, i):
-        return jnp.concatenate(
-            [obs_r[2 * g, i : i + 1, :], obs_r[2 * g + 1, i : i + 1, :]], axis=1
-        )
-
-    lo_iota = lax.broadcasted_iota(jnp.int32, (LANES, 2 * LANES), 0)
-
-    def hot(g):
-        col = lines_of(g, lev).astype(jnp.int32)
-        lo = col & (LANES - 1)
-        block = (col // LANES) & (ens - 1)
-        hi = col // width
-        hi = jnp.where((col >= 0) & (block == e), hi, -1)
-        himask[g] = jnp.broadcast_to(hi, (lev, 2 * LANES))
-        onehot[g] = jnp.where(
-            jnp.broadcast_to(lo, (LANES, 2 * LANES)) == lo_iota, 1.0, 0.0
-        ).astype(BF16)
-
-    loop(pairs, hot)
 
     def smooth(m, center, from_up, from_down):
         for i in range(total_rows):
@@ -356,6 +344,33 @@
         return remote(accb.at[to], rbuf.at[e], s_rs.at[to], r_rs.at[e], to, t)
 
     loop(ens - 1, lambda k: rs_copy(k + 1).start())
+
+    def obs_wait(k):
+        s = peer_t(k + 1)
+        remote(obs_s.at[s], obs_r.at[s], s_obs.at[s], r_obs.at[s], e, s).wait_recv()
+
+    loop(tiles - 1, obs_wait)
+    pairs = tiles // 2
+
+    def lines_of(g, i):
+        return jnp.concatenate(
+            [obs_r[2 * g, i : i + 1, :], obs_r[2 * g + 1, i : i + 1, :]], axis=1
+        )
+
+    lo_iota = lax.broadcasted_iota(jnp.int32, (LANES, 2 * LANES), 0)
+
+    def hot(g):
+        col = lines_of(g, lev).astype(jnp.int32)
+        lo = col & (LANES - 1)
+        block = (col // LANES) & (ens - 1)
+        hi = col // width
+        hi = jnp.where((col >= 0) & (block == e), hi, -1)
+        himask[g] = jnp.broadcast_to(hi, (lev, 2 * LANES))
+        onehot[g] = jnp.where(
+            jnp.broadcast_to(lo, (LANES, 2 * LANES)) == lo_iota, 1.0, 0.0
+        ).astype(BF16)
+
+    loop(pairs, hot)
 
     def rs_wait(k):
         s = peer_e(k + 1)
@@ -424,14 +439,6 @@
     for h in range(hi_n):
         adjf[h] = jnp.concatenate([abuf[b, h] for b in range(ens)], axis=1)
 
-    def force(m):
-        for r in range(rows):
-            ff[m, r] = pp[0, m, r] * adjf[r] + pp[1, m, r] * adjf[rows + r]
-        for copy in halo(m, ff, fu, fd, s_f, r_f):
-            copy.start()
-
-    loop(members, force)
-
     wnd_u[...] = winds(0)[2] * adjf[rows]
     wnd_d[...] = winds(rows - 1)[3] * adjf[2 * rows - 1]
     wind = [
@@ -441,6 +448,14 @@
     for copy in wind:
         copy.start()
 
+    def force(m):
+        for r in range(rows):
+            ff[m, r] = pp[0, m, r] * adjf[r] + pp[1, m, r] * adjf[rows + r]
+        for copy in halo(m, ff, fu, fd, s_f, r_f):
+            copy.start()
+
+    loop(members, force)
+
     def dg_wait(k):
         s = peer_e(k + 1)
         remote(depp, dbuf.at[s], s_dg.at[s], r_dg.at[s], s, t).wait_recv()
@@ -462,15 +477,6 @@
 
     loop(tiles - 1, lambda k: dep_copy(k + 1).start())
     depr[t] = deps[t]
-
-    def backward(m):
-        for copy in halo(m, ff, fu, fd, s_f, r_f):
-            copy.wait_recv()
-        res = smooth(m, ff, fu, fd)
-        for r in range(rows):
-            gens[m, :, r, :] = cc[m, r] + res[NDIFF + r] * fin[r]
-
-    loop(members, backward)
 
     for copy in wind:
         copy.wait_recv()
@@ -489,6 +495,19 @@
         moved = moved + lower - upper
         gsta[:, r, :] = stc[:, r, :] + scale * (adjf[r] + moved)
 
+    def store_of(m):
+        return pltpu.make_async_copy(gens.at[m], gens_hbm.at[m], s_out.at[m])
+
+    def backward(m):
+        for copy in halo(m, ff, fu, fd, s_f, r_f):
+            copy.wait_recv()
+        res = smooth(m, ff, fu, fd)
+        for r in range(rows):
+            gens[m, :, r, :] = cc[m, r] + res[NDIFF + r] * fin[r]
+        store_of(m).start()
+
+    loop(members, backward)
+
     def dep_wait(k):
         s = peer_t(k + 1)
         remote(deps.at[s], depr.at[s], s_dep.at[s], r_dep.at[s], e, s).wait_recv()
@@ -505,6 +524,7 @@
         out = out + jnp.dot(spread1, piece, preferred_element_type=F32)
     gdep[...] = out
 
+    loop(members, lambda m: store_of(m).wait())
     for copy in pre + wind:
         copy.wait_send()
 
@@ -526,6 +546,17 @@
         dg_copy(k + 1).wait_send()
 
     loop(ens - 1, sent_e)
+
+
+def hand_over(x0, x1, x2, y0, y1, y2, sems):
+    copies = [
+        pltpu.make_async_copy(x, y, sems.at[i])
+        for i, (x, y) in enumerate(((x0, y0), (x1, y1), (x2, y2)))
+    ]
+    for copy in copies:
+        copy.start()
+    for copy in copies:
+        copy.wait()
 
 
 def per_device(
@@ -553,6 +584,11 @@
     total_rows = rows + 2 * NDIFF
     fields = (members, rows) + line
     scratch = [
+        vmem(*ens_control.shape),
+        vmem(*perturbations.shape, dtype=BF16),
+        vmem(*ens_control.shape),
+        dma(2),
+        dma(members),
         vmem(tiles, lev, LANES),
         vmem(rows, width),
         vmem(rows, width),
@@ -603,6 +639,7 @@
     ]
     v = pl.BlockSpec(memory_space=pltpu.VMEM)
     s = pl.BlockSpec(memory_space=pltpu.SMEM)
+    a = pl.BlockSpec(memory_space=pl.ANY)
     shape = jax.ShapeDtypeStruct
     grad_ens, grad_static, departures = pl.pallas_call(
         functools.partial(kernel, factor, ens, tiles),
@@ -611,8 +648,8 @@
             shape(static_control.shape, F32),
             shape((tiles, LANES), F32),
         ),
-        in_specs=[v, v, v, s, v, v, v, v, v, v, v, v],
-        out_specs=(v, v, v),
+        in_specs=[a, v, a, s, v, v, v, v, v, v, v, v],
+        out_specs=(a, v, v),
         scratch_shapes=scratch,
         name="gradient",
         compiler_params=pltpu.CompilerParams(
@@ -632,6 +669,14 @@
         obs_weight.reshape(tiles, LANES),
         obs_kernel,
     )
+    grad_ens, grad_static, departures = pl.pallas_call(
+        hand_over,
+        out_shape=tuple(shape(x.shape, F32) for x in (grad_ens, grad_static, departures)),
+        in_specs=[a, a, a],
+        out_specs=(a, a, a),
+        scratch_shapes=[dma(3)],
+        name="results",
+    )(grad_ens, grad_static, departures)
     return (grad_ens, grad_static, departures.reshape(-1))
 
 

time: 98.5 us -> 125 us (1.27)
  Pallas kernels: 94 us -> 124 us
  local copies, waits for them, and re-layouts: 3.63 us -> 0 us
    pallas_call x0 -> x1, Pallas kernels: none -> 37.4 us  [per_device(): pl.pallas_call(hand_over, out_shape=tuple((shape(x.shape, F32) for x in (...]
    pallas_call x1, Pallas kernels: 94 us -> 87 us  [per_device(): pl.pallas_call(functools.partial(kernel, factor, ens, tiles), out_shape=(...]
    unnamed x7 -> x0, local copies, waits for them, and re-layouts: 3.63 us -> none
where the time goes in v2:
time: 125 us
  Pallas kernels  124 us (99%)
    pallas_call x1, Pallas kernels, per_device(): pl.pallas_call(functools.partial(kernel, factor, ens, tiles), out_shape=(...  87 us
    pallas_call x1, Pallas kernels, per_device(): pl.pallas_call(hand_over, out_shape=tuple((shape(x.shape, F32) for x in (...  37.4 us

profile of v2, /device:TPU:1, one launch (start us, length us, event | category | flops | bytes accessed | tf_op | source)
XLA Modules:
  0.0 125.0 jit_solution(15184814298217858446)
XLA Ops:
  0.6 87.0 %gradient.1 = (f32[8,8,4,1024]{3,2,1,0:T(4,128)}, f32[8,4,1024]{2,1,0:T(4,128)}, f32[32,128]{1,0:T(8,128)}) custom-call(f32[8,8,4,1024]{3,2,1,0:T(4,128)} %ctl_hbm.1, f32[8,4,1024]{2,1,0:T(4,128)} %stc.1, bf16[2,8,8,4,1024]{4,3,2,1,0:T(4,128)(2,1)} %per_hbm.1, f32[8]{0:T(128)} %sigma.1, s32[4,1024]{1,0:T(4,128)} %cls.1, f32[4,1024]{1,0:T(4,128)} %east.1, ...), custom_call_target="tpu_custom_call" | custom-call | tf_op jit(solution)/shard_map/gradient/pallas_call | solution.py:644
  87.6 37.4 %results.1 = (f32[8,8,4,1024]{3,2,1,0:T(4,128)}, f32[8,4,1024]{2,1,0:T(4,128)}, f32[32,128]{1,0:T(8,128)}) custom-call(f32[8,8,4,1024]{3,2,1,0:T(4,128)} %get-tuple-element.9.x0, f32[8,4,1024]{2,1,0:T(4,128)} %get-tuple-element.10.x1, f32[32,128]{1,0:T(8,128)} %get-tuple-element.11.x2), custom_call_target="tpu_custom_call" | custom-call | tf_op jit(solution)/shard_map/results/pallas_call | solution.py:672

commit v3 on v2

--- a/solution.py
+++ b/solution.py
@@ -548,14 +548,22 @@
     loop(ens - 1, sent_e)
 
 
-def hand_over(x0, x1, x2, y0, y1, y2, sems):
-    copies = [
-        pltpu.make_async_copy(x, y, sems.at[i])
-        for i, (x, y) in enumerate(((x0, y0), (x1, y1), (x2, y2)))
+def hand_over(x0, x1, x2, y0, y1, y2, b0, b1, b2, s_in, s_out):
+    members = x0.shape[0]
+    triples = [(x0.at[m], b0.at[m], y0.at[m]) for m in range(members)]
+    triples += [(x1, b1, y1), (x2, b2, y2)]
+    come = [
+        pltpu.make_async_copy(x, b, s_in.at[i]) for i, (x, b, y) in enumerate(triples)
     ]
-    for copy in copies:
+    go = [
+        pltpu.make_async_copy(b, y, s_out.at[i]) for i, (x, b, y) in enumerate(triples)
+    ]
+    for copy in come:
         copy.start()
-    for copy in copies:
+    for a, b in zip(come, go):
+        a.wait()
+        b.start()
+    for copy in go:
         copy.wait()
 
 
@@ -674,7 +682,10 @@
         out_shape=tuple(shape(x.shape, F32) for x in (grad_ens, grad_static, departures)),
         in_specs=[a, a, a],
         out_specs=(a, a, a),
-        scratch_shapes=[dma(3)],
+        scratch_shapes=[
+            vmem(*x.shape) for x in (grad_ens, grad_static, departures)
+        ]
+        + [dma(members + 2), dma(members + 2)],
         name="results",
     )(grad_ens, grad_static, departures)
     return (grad_ens, grad_static, departures.reshape(-1))

time: 125 us -> 89.9 us (0.72)
  Pallas kernels: 124 us -> 89.1 us
    pallas_call x1, Pallas kernels: 37.4 us -> 2.17 us  [per_device(): pl.pallas_call(hand_over, out_shape=tuple((shape(x.shape, F32) for x in (...]
where the time goes in v3:
time: 89.9 us; the launch traced here: 89.8 us
  Pallas kernels  89.1 us (99%)
    pallas_call x1, Pallas kernels, per_device(): pl.pallas_call(functools.partial(kernel, factor, ens, tiles), out_shape=(...  87 us
    pallas_call x1, Pallas kernels, per_device(): pl.pallas_call(hand_over, out_shape=tuple((shape(x.shape, F32) for x in (...  2.17 us

profile of v3, /device:TPU:1, one launch (start us, length us, event | category | flops | bytes accessed | tf_op | source)
XLA Modules:
  0.0 89.8 jit_solution(6434644361521520082)
XLA Ops:
  0.6 87.0 %gradient.1 = (f32[8,8,4,1024]{3,2,1,0:T(4,128)}, f32[8,4,1024]{2,1,0:T(4,128)}, f32[32,128]{1,0:T(8,128)}) custom-call(f32[8,8,4,1024]{3,2,1,0:T(4,128)} %ctl_hbm.1, f32[8,4,1024]{2,1,0:T(4,128)} %stc.1, bf16[2,8,8,4,1024]{4,3,2,1,0:T(4,128)(2,1)} %per_hbm.1, f32[8]{0:T(128)} %sigma.1, s32[4,1024]{1,0:T(4,128)} %cls.1, f32[4,1024]{1,0:T(4,128)} %east.1, ...), custom_call_target="tpu_custom_call" | custom-call | tf_op jit(solution)/shard_map/gradient/pallas_call | solution.py:652
  87.6 2.2 %results.1 = (f32[8,8,4,1024]{3,2,1,0:T(4,128)}, f32[8,4,1024]{2,1,0:T(4,128)}, f32[32,128]{1,0:T(8,128)}) custom-call(f32[8,8,4,1024]{3,2,1,0:T(4,128)} %get-tuple-element.9.x0, f32[8,4,1024]{2,1,0:T(4,128)} %get-tuple-element.10.x1, f32[32,128]{1,0:T(8,128)} %get-tuple-element.11.x2), custom_call_target="tpu_custom_call" | custom-call | tf_op jit(solution)/shard_map/results/pallas_call | solution.py:680

commit v4 on v3

--- a/solution.py
+++ b/solution.py
@@ -25,6 +25,11 @@
     b = rest.astype(BF16)
     c = (rest - b.astype(F32)).astype(BF16)
     return a, b, c
+
+
+def split2(x):
+    a = x.astype(BF16).astype(F32)
+    return a, x - a
 
 
 def left(x):
@@ -90,6 +95,14 @@
     obs_r,
     onehot,
     himask,
+    okern,
+    oaux,
+    fe,
+    eu,
+    ed,
+    pk,
+    pk_u,
+    pk_d,
     adjb,
     abuf,
     adjf,
@@ -115,6 +128,8 @@
     r_w,
     s_dep,
     r_dep,
+    s_pk,
+    r_pk,
 ):
     members, lev, rows, width = ctl.shape
     load_ctl = pltpu.make_async_copy(ctl_hbm, ctl, s_in.at[0])
@@ -184,22 +199,29 @@
     for copy in pre:
         copy.start()
 
-    def halo(m, own, from_up, from_down, ssem, rsem):
+    half = width // 2
+    nb = half // LANES
+    edge = NDIFF
+
+    def halo(m, part, own, from_up, from_down, ssem, rsem):
+        cols = pl.ds(part * half, half)
+        src = own.at[m, :, :, cols]
         return (
-            remote(own.at[m], from_up.at[m], ssem.at[0, m], rsem.at[0, m], e, down),
-            remote(own.at[m], from_down.at[m], ssem.at[1, m], rsem.at[1, m], e, up),
+            remote(
+                src, from_up.at[m, :, :, cols], ssem.at[0, part, m], rsem.at[0, part, m], e, down
+            ),
+            remote(
+                src, from_down.at[m, :, :, cols], ssem.at[1, part, m], rsem.at[1, part, m], e, up
+            ),
         )
 
     def send_control(m):
         for r in range(rows):
             cc[m, r] = ctl[m, :, r, :]
-        for copy in halo(m, cc, cu, cd, s_c, r_c):
+        for copy in halo(m, 0, cc, cu, cd, s_c, r_c):
             copy.start()
 
-    def control_part(low, high):
-        lax.fori_loop(low, high, lambda m, c: (send_control(m), c)[1], 0)
-
-    control_part(0, members // 2)
+    loop(members, send_control)
 
     count = jnp.broadcast_to(ocnt[...].astype(F32), (tiles, tiles))
     d_sub = lax.broadcasted_iota(jnp.int32, (tiles, tiles), 0)
@@ -251,7 +273,12 @@
         return remote(obs_s.at[d], obs_r.at[t], s_obs.at[d], r_obs.at[t], e, d)
 
     loop(tiles - 1, lambda k: obs_copy(k + 1).start())
-    control_part(members // 2, members)
+
+    def send_second(m):
+        for copy in halo(m, 1, cc, cu, cd, s_c, r_c):
+            copy.start()
+
+    loop(members, send_second)
     obs_r[t] = obs_s[t]
 
     def spread(m):
@@ -273,10 +300,23 @@
         src = above if i < NDIFF else (own if i < NDIFF + rows else below)
         j = i if i < NDIFF else (i - NDIFF if i < NDIFF + rows else i - NDIFF - rows)
         line = jnp.broadcast_to(src[j : j + 1, :], (lev, width))
-        dbc[i] = line
-        dsq[i] = line * line
+        dbc[i, :, 0:width] = line
+        dsq[i, :, 0:width] = line * line
+        dbc[i, :, width:] = line[:, 0:LANES]
+        dsq[i, :, width:] = line[:, 0:LANES] * line[:, 0:LANES]
         if NDIFF <= i < NDIFF + rows:
-            fin[i - NDIFF] = factor / line
+            fin[i - NDIFF, :, 0:width] = factor / line
+            fin[i - NDIFF, :, width:] = factor / line[:, 0:LANES]
+
+    lane_u = lax.broadcasted_iota(jnp.int32, (lev, LANES), 1)
+
+    def tile_of(x, b):
+        return x[:, b * LANES : (b + 1) * LANES]
+
+    def seam(head, tail):
+        return jnp.where(
+            lane_u < edge, head, jnp.where(lane_u >= LANES - edge, tail, 0.0)
+        )
 
     pre[2].wait_recv()
     pre[3].wait_recv()
@@ -298,147 +338,315 @@
         below = sta[r + 1] if r < rows - 1 else jnp.where(last, 0.0, sta_d[...])
         moved = q - ep * (q - left(q)) - em * (right(q) - q)
         moved = moved - np_ * (q - above) - nm * (below - q)
-        for b in range(ens):
-            stb[b, r] = q[:, b * LANES : (b + 1) * LANES]
-            stb[b, rows + r] = moved[:, b * LANES : (b + 1) * LANES]
-
-    def smooth(m, center, from_up, from_down):
+        for s, value in enumerate((q, moved)):
+            for b in range(nb):
+                stb[s * nb + b, r] = tile_of(value, b)
+                stb[s * nb + b, rows + r] = tile_of(value, nb + b)
+            stb[s * rows + r, 2 * rows] = seam(tile_of(value, 0), tile_of(value, nb - 1))
+
+    window = ((0, half), (half - LANES, width + LANES))
+
+    def band(ref, part, *at):
+        if part == 0:
+            return ref[(*at, slice(None), slice(0, half))]
+        return jnp.concatenate(
+            [
+                ref[(*at, slice(None), slice(half - LANES, width))],
+                ref[(*at, slice(None), slice(0, LANES))],
+            ],
+            axis=1,
+        )
+
+    def band_e(ref, eref, m, r):
+        fix = eref[m, r]
+        return jnp.concatenate(
+            [
+                jnp.where(lane_u >= LANES - edge, fix, ref[m, r, :, half - LANES : half]),
+                ref[m, r, :, half:width],
+                jnp.where(lane_u < edge, fix, ref[m, r, :, 0:LANES]),
+            ],
+            axis=1,
+        )
+
+    def smooth(part, lines):
+        a, b = window[part]
+        n = b - a
         for i in range(total_rows):
-            if i < NDIFF:
-                line = from_up[m, i]
-            elif i < NDIFF + rows:
-                line = center[m, i - NDIFF]
-            else:
-                line = from_down[m, i - NDIFF - rows]
-            wa[i] = dbc[i] * line
+            wa[i, :, 0:n] = dbc[i, :, a:b] * lines(i)
         src, dst = wa, wb
         for step in range(NDIFF):
             for i in range(step + 1, total_rows - 1 - step):
-                w = src[i]
-                lap = src[i + 1] + src[i - 1] + left(w) + right(w) - 4.0 * w
-                dst[i] = w + dsq[i] * lap
+                w = src[i, :, 0:n]
+                lap = src[i + 1, :, 0:n] + src[i - 1, :, 0:n]
+                lap = lap + left(w) + right(w) - 4.0 * w
+                dst[i, :, 0:n] = w + dsq[i, :, a:b] * lap
             src, dst = dst, src
-        return src
-
-    for h in range(hi_n):
-        acc[h] = jnp.zeros((lev, width), F32)
-
-    def forward(m):
-        for copy in halo(m, cc, cu, cd, s_c, r_c):
+        return [src[NDIFF + r, :, 0:n] for r in range(rows)]
+
+    def source_of(i, refs):
+        if i < NDIFF:
+            return refs[0], i
+        if i < NDIFF + rows:
+            return refs[1], i - NDIFF
+        return refs[2], i - NDIFF - rows
+
+    def forward(part, m):
+        for copy in halo(m, part, cc, cu, cd, s_c, r_c):
             copy.wait_recv()
-        res = smooth(m, cc, cu, cd)
+
+        def lines(i):
+            ref, r = source_of(i, (cu, cc, cd))
+            return band(ref, part, m, r)
+
+        n = window[part][1] - window[part][0]
+        res = smooth(part, lines)
         for r in range(rows):
-            w = res[NDIFF + r]
             for s in range(NT):
-                acc[s * rows + r] += pp[s, m, r] * w
-
-    loop(members, forward)
-
-    for h in range(hi_n):
-        value = acc[h] * fin[h % rows]
-        for b in range(ens):
-            accb[b, h] = value[:, b * LANES : (b + 1) * LANES]
-
-    def rs_copy(k):
+                h = s * rows + r
+                acc[h, :, 0:n] = acc[h, :, 0:n] + band(pp, part, s, m, r) * res[r]
+
+    ranges = ((0, rows), (rows, rows + 1))
+
+    def clear():
+        for h in range(hi_n):
+            acc[h] = jnp.zeros(acc.shape[1:], F32)
+
+    def rs_copy(part, k):
         to = peer_e(k)
-        return remote(accb.at[to], rbuf.at[e], s_rs.at[to], r_rs.at[e], to, t)
-
-    loop(ens - 1, lambda k: rs_copy(k + 1).start())
+        first_u, count_u = ranges[part]
+        at = pl.ds(first_u, count_u)
+        return remote(
+            accb.at[to, at], rbuf.at[e, at], s_rs.at[part, to], r_rs.at[part, e], to, t
+        )
+
+    def rs_start(part):
+        a, b = window[part]
+        for s in range(NT):
+            for r in range(rows):
+                h = s * rows + r
+                value = acc[h, :, 0 : b - a] * fin[r, :, a:b]
+                for j in range(nb):
+                    accb[s * nb + j, part * rows + r] = tile_of(value, j + part)
+                if part:
+                    accb[h, 2 * rows] = seam(tile_of(value, nb + 1), tile_of(value, 0))
+        loop(ens - 1, lambda k: rs_copy(part, k + 1).start())
+
+    def rs_wait(part):
+        first_u, count_u = ranges[part]
+        at = pl.ds(first_u, count_u)
+
+        def one(k):
+            s = peer_e(k + 1)
+            remote(
+                accb.at[s, at], rbuf.at[s, at], s_rs.at[part, s], r_rs.at[part, s], s, t
+            ).wait_recv()
+
+        loop(ens - 1, one)
+        for u in range(first_u, first_u + count_u):
+            rbuf[e, u] = accb[e, u]
+
+    group = min(ens, tiles)
+    chunks = tiles // group
 
     def obs_wait(k):
         s = peer_t(k + 1)
         remote(obs_s.at[s], obs_r.at[s], s_obs.at[s], r_obs.at[s], e, s).wait_recv()
 
-    loop(tiles - 1, obs_wait)
-    pairs = tiles // 2
-
-    def lines_of(g, i):
+    def lines_of(g, i, n=1):
         return jnp.concatenate(
-            [obs_r[2 * g, i : i + 1, :], obs_r[2 * g + 1, i : i + 1, :]], axis=1
-        )
-
-    lo_iota = lax.broadcasted_iota(jnp.int32, (LANES, 2 * LANES), 0)
+            [obs_r[group * g + j, i : i + n, :] for j in range(group)], axis=1
+        )
+
+    lo_iota = lax.broadcasted_iota(jnp.int32, (LANES, group * LANES), 0)
+    my_tile = lax.rem(e, nb)
+    my_time = e // nb
 
     def hot(g):
         col = lines_of(g, lev).astype(jnp.int32)
         lo = col & (LANES - 1)
-        block = (col // LANES) & (ens - 1)
+        block = (col // LANES) & (2 * nb - 1)
         hi = col // width
-        hi = jnp.where((col >= 0) & (block == e), hi, -1)
-        himask[g] = jnp.broadcast_to(hi, (lev, 2 * LANES))
+        row = hi & (rows - 1)
+        seams = ((block == 0) & (lo < edge)) | ((block == nb - 1) & (lo >= LANES - edge))
+        mine = ((block & (nb - 1)) == my_tile) & (hi // rows == my_time)
+        unit = jnp.where(mine, jnp.where(block >= nb, rows + row, row), -1)
+        unit = jnp.where(seams, jnp.where(hi == e, 2 * rows, -1), unit)
+        unit = jnp.where(col >= 0, unit, -1)
+        himask[g] = jnp.broadcast_to(unit, (lev, group * LANES))
+        okern[g] = lines_of(g, 0, lev)
+        oaux[g, 0:1, :] = lines_of(g, lev + 1)
+        oaux[g, 1:2, :] = lines_of(g, lev + 2)
         onehot[g] = jnp.where(
-            jnp.broadcast_to(lo, (LANES, 2 * LANES)) == lo_iota, 1.0, 0.0
+            jnp.broadcast_to(lo, (LANES, group * LANES)) == lo_iota, 1.0, 0.0
         ).astype(BF16)
 
-    loop(pairs, hot)
-
-    def rs_wait(k):
-        s = peer_e(k + 1)
-        remote(accb.at[s], rbuf.at[s], s_rs.at[s], r_rs.at[s], s, t).wait_recv()
-
-    loop(ens - 1, rs_wait)
-    rbuf[e] = accb[e]
-    parts = ([], [], [])
-    for h in range(hi_n):
-        value = stb[e, h]
-        for b in range(ens):
-            value = value + rbuf[b, h]
-        for store, piece in zip(parts, split3(value)):
-            store.append(piece)
-    table = jnp.concatenate(parts[0] + parts[1] + parts[2], axis=0)
-    points = hi_n * lev
-
-    def observe(g, total):
-        flat = jnp.dot(table, onehot[g], preferred_element_type=F32)
-        flat = flat[0:points] + flat[points : 2 * points] + flat[2 * points : 3 * points]
-        hi = himask[g]
-        kern = jnp.concatenate(
-            [obs_r[2 * g, 0:lev, :], obs_r[2 * g + 1, 0:lev, :]], axis=1
-        )
-        profile = jnp.zeros((lev, 2 * LANES), F32)
-        for h in range(hi_n):
-            profile = jnp.where(hi == h, flat[h * lev : (h + 1) * lev], profile)
-        evolved = jnp.sum(kern * profile, axis=0, keepdims=True)
-        dep = lines_of(g, lev + 2) * (evolved - lines_of(g, lev + 1))
-        dep = jnp.where(hi[0:1] >= 0, dep, 0.0)
-        depp[2 * g] = dep[:, 0:LANES]
-        depp[2 * g + 1] = dep[:, LANES : 2 * LANES]
-        push = kern * dep
-        place = jnp.concatenate(
-            [jnp.where(hi == h, push, 0.0) for h in range(hi_n)], axis=0
-        )
-        return total + lax.dot_general(
-            jnp.concatenate(split3(place), axis=0),
-            onehot[g],
-            (((1,), (1,)), ((), ())),
-            preferred_element_type=F32,
-        )
-
-    total = lax.fori_loop(0, pairs, observe, jnp.zeros((3 * points, LANES), F32))
-    total = total[0:points] + total[points : 2 * points] + total[2 * points : 3 * points]
-    for h in range(hi_n):
-        adjb[h] = total[h * lev : (h + 1) * lev]
-
-    def ag_copy(k):
+    def observe(part):
+        first_u, count_u = ranges[part]
+        points = count_u * lev
+        values = []
+        for u in range(first_u, first_u + count_u):
+            value = stb[e, u]
+            for b in range(ens):
+                value = value + rbuf[b, u]
+            values.append(value)
+        table = jnp.concatenate(split2(jnp.concatenate(values, axis=0)), axis=0)
+        table = table.astype(BF16)
+        total = jnp.zeros((2 * points, LANES), F32)
+        for g in range(chunks):
+            hi = himask[g]
+            kern = okern[g]
+            flat = jnp.dot(table, onehot[g], preferred_element_type=F32)
+            profile = jnp.zeros(kern.shape, F32)
+            for j in range(count_u):
+                value = flat[j * lev : (j + 1) * lev]
+                value = value + flat[points + j * lev : points + (j + 1) * lev]
+                profile = jnp.where(hi == first_u + j, value, profile)
+            evolved = jnp.sum(kern * profile, axis=0, keepdims=True)
+            dep = oaux[g, 1:2, :] * (evolved - oaux[g, 0:1, :])
+            inside = (hi[0:1] >= first_u) & (hi[0:1] < first_u + count_u)
+            dep = jnp.where(inside, dep, 0.0)
+            for j in range(group):
+                piece = dep[:, j * LANES : (j + 1) * LANES]
+                depp[group * g + j] = piece if part == 0 else depp[group * g + j] + piece
+            push = kern * dep
+            place = jnp.concatenate(
+                [jnp.where(hi == first_u + j, push, 0.0) for j in range(count_u)], axis=0
+            )
+            place = jnp.concatenate(split2(place), axis=0).astype(BF16)
+            total = total + lax.dot_general(
+                place, onehot[g], (((1,), (1,)), ((), ())), preferred_element_type=F32
+            )
+        total = total[0:points] + total[points : 2 * points]
+        for j in range(count_u):
+            adjb[first_u + j] = total[j * lev : (j + 1) * lev]
+            abuf[e, first_u + j] = total[j * lev : (j + 1) * lev]
+        loop(ens - 1, lambda k: ag_copy(part, k + 1).start())
+
+    def ag_copy(part, k):
         to = peer_e(k)
-        return remote(adjb, abuf.at[e], s_ag.at[to], r_ag.at[e], to, t)
+        at = pl.ds(*ranges[part])
+        return remote(
+            adjb.at[at], abuf.at[e, at], s_ag.at[part, to], r_ag.at[part, e], to, t
+        )
+
+    def ag_wait(part):
+        at = pl.ds(*ranges[part])
+
+        def one(k):
+            s = peer_e(k + 1)
+            remote(
+                adjb.at[at], abuf.at[s, at], s_ag.at[part, s], r_ag.at[part, s], s, t
+            ).wait_recv()
+
+        loop(ens - 1, one)
+        for s in range(NT):
+            for r in range(rows):
+                adjf[s * rows + r, :, part * half : (part + 1) * half] = jnp.concatenate(
+                    [abuf[s * nb + b, part * rows + r] for b in range(nb)], axis=1
+                )
 
     def dg_copy(k):
         to = peer_e(k)
         return remote(depp, dbuf.at[e], s_dg.at[to], r_dg.at[e], to, t)
 
-    loop(ens - 1, lambda k: ag_copy(k + 1).start())
+    def force(part, m):
+        a, b = part * half, (part + 1) * half
+        for r in range(rows):
+            ff[m, r, :, a:b] = (
+                pp[0, m, r, :, a:b] * adjf[r, :, a:b]
+                + pp[1, m, r, :, a:b] * adjf[rows + r, :, a:b]
+            )
+        for copy in halo(m, part, ff, fu, fd, s_f, r_f):
+            copy.start()
+
+    def force_seams(m):
+        for r in range(rows):
+            head = (
+                pp[0, m, r, :, 0:LANES] * abuf[r, 2 * rows]
+                + pp[1, m, r, :, 0:LANES] * abuf[rows + r, 2 * rows]
+            )
+            tail = (
+                pp[0, m, r, :, half - LANES : half] * abuf[r, 2 * rows]
+                + pp[1, m, r, :, half - LANES : half] * abuf[rows + r, 2 * rows]
+            )
+            fe[m, r] = seam(head, tail)
+
+    def backward_first(m):
+        for copy in halo(m, 0, ff, fu, fd, s_f, r_f):
+            copy.wait_recv()
+
+        def lines(i):
+            ref, r = source_of(i, (fu, ff, fd))
+            return ref[m, r, :, 0:half]
+
+        res = smooth(0, lines)
+        for r in range(rows):
+            gens[m, :, r, 0:half] = cc[m, r, :, 0:half] + res[r] * fin[r, :, 0:half]
+
+    def store_of(m):
+        return pltpu.make_async_copy(gens.at[m], gens_hbm.at[m], s_out.at[m])
+
+    def backward_second(m):
+        for copy in halo(m, 1, ff, fu, fd, s_f, r_f):
+            copy.wait_recv()
+
+        def lines(i):
+            (ref, eref), r = source_of(i, ((fu, eu), (ff, fe), (fd, ed)))
+            return band_e(ref, eref, m, r)
+
+        res = smooth(1, lines)
+        a, b = window[1]
+        for r in range(rows):
+            value = res[r] * fin[r, :, a:b] + band(cc, 1, m, r)
+            gens[m, :, r, half:width] = value[:, LANES : LANES + half]
+            gens[m, :, r, half - LANES : half] = jnp.where(
+                lane_u >= LANES - 2 * edge, value[:, 0:LANES], gens[m, :, r, half - LANES : half]
+            )
+            gens[m, :, r, 0:LANES] = jnp.where(
+                lane_u < 2 * edge, value[:, LANES + half :], gens[m, :, r, 0:LANES]
+            )
+        store_of(m).start()
+
+    clear()
+    loop(members, functools.partial(forward, 0))
+    rs_start(0)
+    clear()
+    loop(tiles - 1, obs_wait)
+    for g in range(chunks):
+        hot(g)
+    rs_wait(0)
+    observe(0)
+    loop(members, functools.partial(forward, 1))
+    rs_start(1)
+    ag_wait(0)
+    loop(members, functools.partial(force, 0))
+    rs_wait(1)
+    observe(1)
     loop(ens - 1, lambda k: dg_copy(k + 1).start())
-    abuf[e] = adjb[...]
-
-    def ag_wait(k):
-        s = peer_e(k + 1)
-        remote(adjb, abuf.at[s], s_ag.at[s], r_ag.at[s], s, t).wait_recv()
-
-    loop(ens - 1, ag_wait)
+    early = members // 4
+    loop(early, backward_first)
+    ag_wait(1)
     for h in range(hi_n):
-        adjf[h] = jnp.concatenate([abuf[b, h] for b in range(ens)], axis=1)
-
+        fix = abuf[h, 2 * rows]
+        adjf[h, :, 0:LANES] = adjf[h, :, 0:LANES] + jnp.where(lane_u < edge, fix, 0.0)
+        adjf[h, :, half - LANES : half] = adjf[h, :, half - LANES : half] + jnp.where(
+            lane_u >= LANES - edge, fix, 0.0
+        )
+
+    loop(members, force_seams)
+    each = 2 * edge
+    for r in range(rows):
+        value = jnp.zeros((lev, LANES), F32)
+        for m in range(members):
+            spot = (lane_u >= m * each) & (lane_u < (m + 1) * each)
+            value = jnp.where(spot, pltpu.roll(fe[m, r], edge + m * each, 1), value)
+        pk[r] = value
+    seams = [
+        remote(pk, pk_u, s_pk.at[0], r_pk.at[0], e, down),
+        remote(pk, pk_d, s_pk.at[1], r_pk.at[1], e, up),
+    ]
+    for copy in seams:
+        copy.start()
     wnd_u[...] = winds(0)[2] * adjf[rows]
     wnd_d[...] = winds(rows - 1)[3] * adjf[2 * rows - 1]
     wind = [
@@ -448,13 +656,7 @@
     for copy in wind:
         copy.start()
 
-    def force(m):
-        for r in range(rows):
-            ff[m, r] = pp[0, m, r] * adjf[r] + pp[1, m, r] * adjf[rows + r]
-        for copy in halo(m, ff, fu, fd, s_f, r_f):
-            copy.start()
-
-    loop(members, force)
+    loop(members, functools.partial(force, 1))
 
     def dg_wait(k):
         s = peer_e(k + 1)
@@ -495,18 +697,15 @@
         moved = moved + lower - upper
         gsta[:, r, :] = stc[:, r, :] + scale * (adjf[r] + moved)
 
-    def store_of(m):
-        return pltpu.make_async_copy(gens.at[m], gens_hbm.at[m], s_out.at[m])
-
-    def backward(m):
-        for copy in halo(m, ff, fu, fd, s_f, r_f):
-            copy.wait_recv()
-        res = smooth(m, ff, fu, fd)
+    lax.fori_loop(early, members, lambda m, c: (backward_first(m), c)[1], 0)
+    for copy in seams:
+        copy.wait_recv()
+    for m in range(members):
         for r in range(rows):
-            gens[m, :, r, :] = cc[m, r] + res[NDIFF + r] * fin[r]
-        store_of(m).start()
-
-    loop(members, backward)
+            by = LANES - edge - m * each
+            eu[m, r] = pltpu.roll(pk_u[r], by, 1)
+            ed[m, r] = pltpu.roll(pk_d[r], by, 1)
+    loop(members, backward_second)
 
     def dep_wait(k):
         s = peer_t(k + 1)
@@ -525,12 +724,15 @@
     gdep[...] = out
 
     loop(members, lambda m: store_of(m).wait())
-    for copy in pre + wind:
+    for copy in pre + wind + seams:
         copy.wait_send()
 
     def sent(m):
-        for copy in halo(m, cc, cu, cd, s_c, r_c) + halo(m, ff, fu, fd, s_f, r_f):
-            copy.wait_send()
+        for part in range(2):
+            for copy in halo(m, part, cc, cu, cd, s_c, r_c):
+                copy.wait_send()
+            for copy in halo(m, part, ff, fu, fd, s_f, r_f):
+                copy.wait_send()
 
     loop(members, sent)
 
@@ -541,8 +743,9 @@
     loop(tiles - 1, sent_t)
 
     def sent_e(k):
-        rs_copy(k + 1).wait_send()
-        ag_copy(k + 1).wait_send()
+        for part in range(2):
+            rs_copy(part, k + 1).wait_send()
+            ag_copy(part, k + 1).wait_send()
         dg_copy(k + 1).wait_send()
 
     loop(ens - 1, sent_e)
@@ -589,6 +792,11 @@
     vmem = lambda *shape, dtype=F32: pltpu.VMEM(shape, dtype)
     dma = lambda *shape: pltpu.SemaphoreType.DMA(shape)
     line = (lev, width)
+    wide = width + LANES
+    band = width // 2 + 2 * LANES
+    units = 2 * rows + 1
+    chunks = max(1, tiles // ens)
+    slots = min(ens, tiles) * LANES
     total_rows = rows + 2 * NDIFF
     fields = (members, rows) + line
     scratch = [
@@ -601,13 +809,13 @@
         vmem(rows, width),
         vmem(rows, width),
         vmem(rows, width),
-        vmem(total_rows, *line),
-        vmem(total_rows, *line),
-        vmem(rows, *line),
+        vmem(total_rows, lev, wide),
+        vmem(total_rows, lev, wide),
+        vmem(rows, lev, wide),
         vmem(rows, *line),
         vmem(*line),
         vmem(*line),
-        vmem(ens, hi_n, lev, LANES),
+        vmem(ens, units, lev, LANES),
         vmem(*line),
         vmem(*line),
         vmem(*line),
@@ -619,31 +827,40 @@
         vmem(*fields),
         vmem(*fields),
         vmem(*fields),
-        vmem(total_rows, *line),
-        vmem(total_rows, *line),
-        vmem(hi_n, *line),
-        vmem(ens, hi_n, lev, LANES),
-        vmem(ens, hi_n, lev, LANES),
+        vmem(total_rows, lev, band),
+        vmem(total_rows, lev, band),
+        vmem(hi_n, lev, band),
+        vmem(ens, units, lev, LANES),
+        vmem(ens, units, lev, LANES),
         vmem(tiles, 2 * lev, LANES),
         vmem(tiles, 2 * lev, LANES),
-        vmem(tiles // 2, LANES, 2 * LANES, dtype=BF16),
-        vmem(tiles // 2, lev, 2 * LANES, dtype=jnp.int32),
-        vmem(hi_n, lev, LANES),
-        vmem(ens, hi_n, lev, LANES),
+        vmem(chunks, LANES, slots, dtype=BF16),
+        vmem(chunks, lev, slots, dtype=jnp.int32),
+        vmem(chunks, lev, slots),
+        vmem(chunks, lev, slots),
+        vmem(members, rows, lev, LANES),
+        vmem(members, rows, lev, LANES),
+        vmem(members, rows, lev, LANES),
+        vmem(rows, lev, LANES),
+        vmem(rows, lev, LANES),
+        vmem(rows, lev, LANES),
+        vmem(units, lev, LANES),
+        vmem(ens, units, lev, LANES),
         vmem(hi_n, *line),
         vmem(tiles, 1, LANES),
         vmem(ens, tiles, 1, LANES),
         vmem(tiles, 1, LANES),
         vmem(tiles, 1, LANES),
         dma(4), dma(4),
-        dma(2, members), dma(2, members),
-        dma(2, members), dma(2, members),
+        dma(2, 2, members), dma(2, 2, members),
+        dma(2, 2, members), dma(2, 2, members),
         dma(tiles), dma(tiles),
-        dma(ens), dma(ens),
-        dma(ens), dma(ens),
+        dma(2, ens), dma(2, ens),
+        dma(2, ens), dma(2, ens),
         dma(ens), dma(ens),
         dma(2), dma(2),
         dma(tiles), dma(tiles),
+        dma(2), dma(2),
     ]
     v = pl.BlockSpec(memory_space=pltpu.VMEM)
     s = pl.BlockSpec(memory_space=pltpu.SMEM)

time: 89.9 us -> 90.2 us (level)
  no operation moved by 1% of the time
where the time goes in v4:
time: 90.2 us; the launch traced here: 90.1 us
  Pallas kernels  89.4 us (99%)
    pallas_call x1, Pallas kernels, per_device(): pl.pallas_call(functools.partial(kernel, factor, ens, tiles), out_shape=(...  87.3 us
    pallas_call x1, Pallas kernels, per_device(): pl.pallas_call(hand_over, out_shape=tuple((shape(x.shape, F32) for x in (...  2.17 us

profile of v4, /device:TPU:1, one launch (start us, length us, event | category | flops | bytes accessed | tf_op | source)
XLA Modules:
  0.0 90.1 jit_solution(16920316207803233957)
XLA Ops:
  0.6 87.3 %gradient.1 = (f32[8,8,4,1024]{3,2,1,0:T(4,128)}, f32[8,4,1024]{2,1,0:T(4,128)}, f32[32,128]{1,0:T(8,128)}) custom-call(f32[8,8,4,1024]{3,2,1,0:T(4,128)} %ctl_hbm.1, f32[8,4,1024]{2,1,0:T(4,128)} %stc.1, bf16[2,8,8,4,1024]{4,3,2,1,0:T(4,128)(2,1)} %per_hbm.1, f32[8]{0:T(128)} %sigma.1, s32[4,1024]{1,0:T(4,128)} %cls.1, f32[4,1024]{1,0:T(4,128)} %east.1, ...), custom_call_target="tpu_custom_call" | custom-call | tf_op jit(solution)/shard_map/gradient/pallas_call | solution.py:869
  87.9 2.2 %results.1 = (f32[8,8,4,1024]{3,2,1,0:T(4,128)}, f32[8,4,1024]{2,1,0:T(4,128)}, f32[32,128]{1,0:T(8,128)}) custom-call(f32[8,8,4,1024]{3,2,1,0:T(4,128)} %get-tuple-element.9.x0, f32[8,4,1024]{2,1,0:T(4,128)} %get-tuple-element.10.x1, f32[32,128]{1,0:T(8,128)} %get-tuple-element.11.x2), custom_call_target="tpu_custom_call" | custom-call | tf_op jit(solution)/shard_map/results/pallas_call | solution.py:897

commit v5 on v4

--- a/solution.py
+++ b/solution.py
@@ -91,6 +91,8 @@
     acc,
     accb,
     rbuf,
+    xs,
+    xr,
     obs_s,
     obs_r,
     onehot,
@@ -107,9 +109,12 @@
     abuf,
     adjf,
     depp,
+    depx,
+    dx,
     dbuf,
     deps,
     depr,
+    depf,
     s_pre,
     r_pre,
     s_c,
@@ -130,6 +135,16 @@
     r_dep,
     s_pk,
     r_pk,
+    s_o2,
+    r_o2,
+    s_rx,
+    r_rx,
+    s_ax,
+    r_ax,
+    s_dx,
+    r_dx,
+    s_d2,
+    r_d2,
 ):
     members, lev, rows, width = ctl.shape
     load_ctl = pltpu.make_async_copy(ctl_hbm, ctl, s_in.at[0])
@@ -139,6 +154,13 @@
     hi_n = NT * rows
     e = lax.axis_index("ens")
     t = lax.axis_index("tile")
+    ny = ens // 2
+    y = e // 2
+    xl = lax.rem(e, 2)
+    partner = 2 * y + 1 - xl
+    group = tiles // ny
+    kin = lax.rem(y - lax.rem(t, ny) + ny, ny)
+    line_t = t // ny
     up = lax.rem(t + tiles - 1, tiles)
     down = lax.rem(t + 1, tiles)
     first = t == 0
@@ -161,25 +183,36 @@
 
         lax.fori_loop(0, n, step, 0)
 
-    def peer_e(k):
-        return lax.rem(e + k, ens)
-
-    def peer_t(k):
-        return lax.rem(t + k, tiles)
+    def span(low, high, body):
+        def step(i, carry):
+            body(i)
+            return carry
+
+        lax.fori_loop(low, high, step, 0)
+
+    def peer_y(k):
+        return lax.rem(y + k, ny)
+
+    def each_y(body):
+        span(1, ny, lambda k: body(peer_y(k)))
+
+    def each_kin(body):
+        def one(j):
+            pl.when(j * ny + kin != t)(lambda: body(j, j * ny + kin))
+
+        loop(group, one)
 
     barrier = pltpu.get_barrier_semaphore()
-    loop(
-        tiles - 1,
-        lambda k: pl.semaphore_signal(
-            barrier, inc=1, device_id=(e, peer_t(k + 1)), device_id_type=MESH
-        ),
-    )
-    loop(
-        ens - 1,
-        lambda k: pl.semaphore_signal(
-            barrier, inc=1, device_id=(peer_e(k + 1), t), device_id_type=MESH
-        ),
-    )
+
+    def greet(e_to, t_to):
+        pl.semaphore_signal(barrier, inc=1, device_id=(e_to, t_to), device_id_type=MESH)
+
+    greet(e, up)
+    greet(e, down)
+    each_kin(lambda j, d: greet(e, d))
+    each_y(lambda b: greet(2 * b + xl, t))
+    greet(partner, t)
+    alone = jnp.where(kin == lax.rem(t, ny), 1, 0)
     dif[...] = jnp.sqrt(DIFF_BASE * (cls[...].astype(F32) + 1.0))
     sub = lax.broadcasted_iota(jnp.int32, (lev, width), 0)
     scale = jnp.zeros((lev, width), F32)
@@ -188,7 +221,7 @@
     for r in range(rows):
         sta[r] = scale * stc[:, r, :]
     load_ctl.wait()
-    pl.semaphore_wait(barrier, tiles - 1 + ens - 1)
+    pl.semaphore_wait(barrier, 2 + group - alone + ny)
 
     pre = [
         remote(dif, dif_u, s_pre.at[0], r_pre.at[0], e, down),
@@ -204,24 +237,21 @@
     edge = NDIFF
 
     def halo(m, part, own, from_up, from_down, ssem, rsem):
-        cols = pl.ds(part * half, half)
-        src = own.at[m, :, :, cols]
+        src = own.at[m, part]
         return (
-            remote(
-                src, from_up.at[m, :, :, cols], ssem.at[0, part, m], rsem.at[0, part, m], e, down
-            ),
-            remote(
-                src, from_down.at[m, :, :, cols], ssem.at[1, part, m], rsem.at[1, part, m], e, up
-            ),
+            remote(src, from_up.at[m, part], ssem.at[0, part, m], rsem.at[0, part, m], e, down),
+            remote(src, from_down.at[m, part], ssem.at[1, part, m], rsem.at[1, part, m], e, up),
         )
 
     def send_control(m):
         for r in range(rows):
-            cc[m, r] = ctl[m, :, r, :]
+            for part in range(2):
+                cc[m, part, r] = ctl[m, :, r, part * half : (part + 1) * half]
         for copy in halo(m, 0, cc, cu, cd, s_c, r_c):
             copy.start()
 
-    loop(members, send_control)
+    ahead = members // 4
+    span(0, ahead, send_control)
 
     count = jnp.broadcast_to(ocnt[...].astype(F32), (tiles, tiles))
     d_sub = lax.broadcasted_iota(jnp.int32, (tiles, tiles), 0)
@@ -235,20 +265,35 @@
         axis=0,
         keepdims=True,
     )
-    begin = jnp.broadcast_to(start_col, (tiles, LANES)).astype(jnp.int32)
-    shift = begin & (LANES - 1)
-    lane = lax.broadcasted_iota(jnp.int32, (tiles, LANES), 1)
-    usable = lane < jnp.broadcast_to(count_col, (tiles, LANES)).astype(jnp.int32)
-
-    def turn(x, back):
+    def places(start_of, count_of):
+        shape = (start_of.shape[0], LANES)
+        begin = jnp.broadcast_to(start_of, shape).astype(jnp.int32)
+        lane = lax.broadcasted_iota(jnp.int32, shape, 1)
+        usable = lane < jnp.broadcast_to(count_of, shape).astype(jnp.int32)
+        return lane, begin & (LANES - 1), usable
+
+    def turn(x, shift, back):
         for bit in range(LANES.bit_length() - 1):
             by = LANES - (1 << bit) if back else 1 << bit
             x = jnp.where(shift & (1 << bit) != 0, pltpu.roll(x, by, 1), x)
         return x
 
-    line_col = jnp.broadcast_to(start_col, (tiles, tiles)).astype(jnp.int32) // LANES
+    kin_count = jnp.broadcast_to(ocnt[...].astype(F32), (group, tiles))
+    kin_sub = lax.broadcasted_iota(jnp.int32, (group, tiles), 0) * ny + kin
+    kin_lane = lax.broadcasted_iota(jnp.int32, (group, tiles), 1)
+    kin_start = jnp.sum(
+        jnp.where(kin_lane < kin_sub, kin_count, 0.0), axis=1, keepdims=True
+    )
+    kin_own = jnp.sum(
+        jnp.where(kin_lane == kin_sub, kin_count, 0.0), axis=1, keepdims=True
+    )
+    lane, shift, usable = places(kin_start, kin_own)
+    line_col = jnp.broadcast_to(kin_start, (group, tiles)).astype(jnp.int32) // LANES
     pick = jnp.concatenate(
-        [jnp.where(d_lane == line_col, 1.0, 0.0), jnp.where(d_lane == line_col + 1, 1.0, 0.0)],
+        [
+            jnp.where(kin_lane == line_col, 1.0, 0.0),
+            jnp.where(kin_lane == line_col + 1, 1.0, 0.0),
+        ],
         axis=0,
     ).astype(BF16)
     for b in range(tiles):
@@ -261,25 +306,48 @@
         two = sum(
             jnp.dot(pick, piece, preferred_element_type=F32) for piece in split3(part)
         )
-        value = turn(jnp.where(lane >= shift, two[0:tiles], two[tiles : 2 * tiles]), True)
+        value = jnp.where(lane >= shift, two[0:group], two[group : 2 * group])
+        value = turn(value, shift, True)
         if q == lev:
             value = jnp.where(usable, value, -1.0)
         obs_s[:, q, :] = value
     for q in range(lev + 3, 2 * lev):
-        obs_s[:, q, :] = jnp.zeros((tiles, LANES), F32)
-
-    def obs_copy(k):
-        d = peer_t(k)
-        return remote(obs_s.at[d], obs_r.at[t], s_obs.at[d], r_obs.at[t], e, d)
-
-    loop(tiles - 1, lambda k: obs_copy(k + 1).start())
+        obs_s[:, q, :] = jnp.zeros((group, LANES), F32)
+
+    def obs_copy(j, d):
+        return remote(
+            obs_s.at[j], obs_r.at[y, line_t], s_obs.at[j], r_obs.at[line_t], e, d
+        )
+
+    each_kin(lambda j, d: obs_copy(j, d).start())
+
+    @pl.when(alone == 1)
+    def _():
+        obs_r[y, line_t] = obs_s[line_t]
+
+    span(ahead, members, send_control)
 
     def send_second(m):
         for copy in halo(m, 1, cc, cu, cd, s_c, r_c):
             copy.start()
 
-    loop(members, send_second)
-    obs_r[t] = obs_s[t]
+    def obs_on(b):
+        return remote(obs_r.at[y], obs_r.at[y], s_o2.at[b], r_o2.at[y], 2 * b + xl, t)
+
+    def obs_mid():
+        each_kin(
+            lambda j, d: remote(
+                obs_s.at[j], obs_r.at[y, j], s_obs.at[j], r_obs.at[j], e, d
+            ).wait_recv()
+        )
+        each_y(lambda b: obs_on(b).start())
+
+    def obs_wait():
+        each_y(
+            lambda b: remote(
+                obs_r.at[b], obs_r.at[b], s_o2.at[b], r_o2.at[b], 2 * b + xl, t
+            ).wait_recv()
+        )
 
     def spread(m):
         for s in range(NT):
@@ -346,24 +414,32 @@
 
     window = ((0, half), (half - LANES, width + LANES))
 
-    def band(ref, part, *at):
+    def band(ref, part, m, r):
         if part == 0:
-            return ref[(*at, slice(None), slice(0, half))]
+            return ref[m, 0, r]
         return jnp.concatenate(
             [
-                ref[(*at, slice(None), slice(half - LANES, width))],
-                ref[(*at, slice(None), slice(0, LANES))],
+                ref[m, 0, r, :, half - LANES : half],
+                ref[m, 1, r],
+                ref[m, 0, r, :, 0:LANES],
             ],
             axis=1,
+        )
+
+    def band_p(s, part, m, r):
+        if part == 0:
+            return pp[s, m, r, :, 0:half]
+        return jnp.concatenate(
+            [pp[s, m, r, :, half - LANES : width], pp[s, m, r, :, 0:LANES]], axis=1
         )
 
     def band_e(ref, eref, m, r):
         fix = eref[m, r]
         return jnp.concatenate(
             [
-                jnp.where(lane_u >= LANES - edge, fix, ref[m, r, :, half - LANES : half]),
-                ref[m, r, :, half:width],
-                jnp.where(lane_u < edge, fix, ref[m, r, :, 0:LANES]),
+                jnp.where(lane_u >= LANES - edge, fix, ref[m, 0, r, :, half - LANES : half]),
+                ref[m, 1, r],
+                jnp.where(lane_u < edge, fix, ref[m, 0, r, :, 0:LANES]),
             ],
             axis=1,
         )
@@ -403,7 +479,7 @@
         for r in range(rows):
             for s in range(NT):
                 h = s * rows + r
-                acc[h, :, 0:n] = acc[h, :, 0:n] + band(pp, part, s, m, r) * res[r]
+                acc[h, :, 0:n] = acc[h, :, 0:n] + band_p(s, part, m, r) * res[r]
 
     ranges = ((0, rows), (rows, rows + 1))
 
@@ -411,13 +487,20 @@
         for h in range(hi_n):
             acc[h] = jnp.zeros(acc.shape[1:], F32)
 
-    def rs_copy(part, k):
-        to = peer_e(k)
-        first_u, count_u = ranges[part]
-        at = pl.ds(first_u, count_u)
+    def rs_copy(part, b):
+        at = pl.ds(*ranges[part])
         return remote(
-            accb.at[to, at], rbuf.at[e, at], s_rs.at[part, to], r_rs.at[part, e], to, t
-        )
+            accb.at[pl.ds(2 * b, 2), at],
+            rbuf.at[y, :, at],
+            s_rs.at[part, b],
+            r_rs.at[part, y],
+            2 * b + xl,
+            t,
+        )
+
+    def rx_copy(part):
+        at = pl.ds(*ranges[part])
+        return remote(xs.at[at], xr.at[at], s_rx.at[part], r_rx.at[part], partner, t)
 
     def rs_start(part):
         a, b = window[part]
@@ -429,32 +512,35 @@
                     accb[s * nb + j, part * rows + r] = tile_of(value, j + part)
                 if part:
                     accb[h, 2 * rows] = seam(tile_of(value, nb + 1), tile_of(value, 0))
-        loop(ens - 1, lambda k: rs_copy(part, k + 1).start())
-
-    def rs_wait(part):
+        each_y(lambda b: rs_copy(part, b).start())
+
+    def rs_mid(part):
         first_u, count_u = ranges[part]
         at = pl.ds(first_u, count_u)
-
-        def one(k):
-            s = peer_e(k + 1)
-            remote(
-                accb.at[s, at], rbuf.at[s, at], s_rs.at[part, s], r_rs.at[part, s], s, t
+        each_y(
+            lambda b: remote(
+                accb.at[pl.ds(2 * b, 2), at],
+                rbuf.at[b, :, at],
+                s_rs.at[part, b],
+                r_rs.at[part, b],
+                2 * b + xl,
+                t,
             ).wait_recv()
-
-        loop(ens - 1, one)
+        )
         for u in range(first_u, first_u + count_u):
-            rbuf[e, u] = accb[e, u]
-
-    group = min(ens, tiles)
-    chunks = tiles // group
-
-    def obs_wait(k):
-        s = peer_t(k + 1)
-        remote(obs_s.at[s], obs_r.at[s], s_obs.at[s], r_obs.at[s], e, s).wait_recv()
+            for x in range(2):
+                rbuf[y, x, u] = accb[2 * y + x, u]
+            value = rbuf[0, 1 - xl, u]
+            for b in range(1, ny):
+                value = value + rbuf[b, 1 - xl, u]
+            xs[u] = value
+        rx_copy(part).start()
+
+    chunks = ny
 
     def lines_of(g, i, n=1):
         return jnp.concatenate(
-            [obs_r[group * g + j, i : i + n, :] for j in range(group)], axis=1
+            [obs_r[g, j, i : i + n, :] for j in range(group)], axis=1
         )
 
     lo_iota = lax.broadcasted_iota(jnp.int32, (LANES, group * LANES), 0)
@@ -483,11 +569,12 @@
     def observe(part):
         first_u, count_u = ranges[part]
         points = count_u * lev
+        rx_copy(part).wait_recv()
         values = []
         for u in range(first_u, first_u + count_u):
-            value = stb[e, u]
-            for b in range(ens):
-                value = value + rbuf[b, u]
+            value = stb[e, u] + xr[u]
+            for b in range(ny):
+                value = value + rbuf[b, xl, u]
             values.append(value)
         table = jnp.concatenate(split2(jnp.concatenate(values, axis=0)), axis=0)
         table = table.astype(BF16)
@@ -507,7 +594,7 @@
             dep = jnp.where(inside, dep, 0.0)
             for j in range(group):
                 piece = dep[:, j * LANES : (j + 1) * LANES]
-                depp[group * g + j] = piece if part == 0 else depp[group * g + j] + piece
+                depp[g, j] = piece if part == 0 else depp[g, j] + piece
             push = kern * dep
             place = jnp.concatenate(
                 [jnp.where(hi == first_u + j, push, 0.0) for j in range(count_u)], axis=0
@@ -520,39 +607,53 @@
         for j in range(count_u):
             adjb[first_u + j] = total[j * lev : (j + 1) * lev]
             abuf[e, first_u + j] = total[j * lev : (j + 1) * lev]
-        loop(ens - 1, lambda k: ag_copy(part, k + 1).start())
-
-    def ag_copy(part, k):
-        to = peer_e(k)
+        ax_copy(part).start()
+
+    def ax_copy(part):
         at = pl.ds(*ranges[part])
         return remote(
-            adjb.at[at], abuf.at[e, at], s_ag.at[part, to], r_ag.at[part, e], to, t
-        )
+            adjb.at[at], abuf.at[e, at], s_ax.at[part], r_ax.at[part], partner, t
+        )
+
+    def ag_copy(part, b):
+        here = abuf.at[pl.ds(2 * y, 2), pl.ds(*ranges[part])]
+        return remote(here, here, s_ag.at[part, b], r_ag.at[part, y], 2 * b + xl, t)
+
+    def ag_mid(part):
+        at = pl.ds(*ranges[part])
+        remote(
+            adjb.at[at], abuf.at[partner, at], s_ax.at[part], r_ax.at[part], partner, t
+        ).wait_recv()
+        each_y(lambda b: ag_copy(part, b).start())
 
     def ag_wait(part):
-        at = pl.ds(*ranges[part])
-
-        def one(k):
-            s = peer_e(k + 1)
+        def one(b):
+            there = abuf.at[pl.ds(2 * b, 2), pl.ds(*ranges[part])]
             remote(
-                adjb.at[at], abuf.at[s, at], s_ag.at[part, s], r_ag.at[part, s], s, t
+                there, there, s_ag.at[part, b], r_ag.at[part, b], 2 * b + xl, t
             ).wait_recv()
 
-        loop(ens - 1, one)
+        each_y(one)
         for s in range(NT):
             for r in range(rows):
                 adjf[s * rows + r, :, part * half : (part + 1) * half] = jnp.concatenate(
                     [abuf[s * nb + b, part * rows + r] for b in range(nb)], axis=1
                 )
 
-    def dg_copy(k):
-        to = peer_e(k)
-        return remote(depp, dbuf.at[e], s_dg.at[to], r_dg.at[e], to, t)
+    dx_copy = remote(depp, dx, s_dx.at[0], r_dx.at[0], partner, t)
+
+    def dg_copy(b):
+        return remote(depx, dbuf.at[y], s_dg.at[b], r_dg.at[y], 2 * b + xl, t)
+
+    def dg_mid():
+        dx_copy.wait_recv()
+        depx[...] = depp[...] + dx[...]
+        each_y(lambda b: dg_copy(b).start())
 
     def force(part, m):
         a, b = part * half, (part + 1) * half
         for r in range(rows):
-            ff[m, r, :, a:b] = (
+            ff[m, part, r] = (
                 pp[0, m, r, :, a:b] * adjf[r, :, a:b]
                 + pp[1, m, r, :, a:b] * adjf[rows + r, :, a:b]
             )
@@ -577,11 +678,11 @@
 
         def lines(i):
             ref, r = source_of(i, (fu, ff, fd))
-            return ref[m, r, :, 0:half]
+            return ref[m, 0, r]
 
         res = smooth(0, lines)
         for r in range(rows):
-            gens[m, :, r, 0:half] = cc[m, r, :, 0:half] + res[r] * fin[r, :, 0:half]
+            gens[m, :, r, 0:half] = cc[m, 0, r] + res[r] * fin[r, :, 0:half]
 
     def store_of(m):
         return pltpu.make_async_copy(gens.at[m], gens_hbm.at[m], s_out.at[m])
@@ -607,22 +708,39 @@
             )
         store_of(m).start()
 
+    q1, q2 = members // 4, members * 5 // 8
     clear()
-    loop(members, functools.partial(forward, 0))
+    span(0, members - q1, functools.partial(forward, 0))
+    obs_mid()
+    span(0, q1, send_second)
+    span(members - q1, members, functools.partial(forward, 0))
     rs_start(0)
+    span(q1, q1 + 1, send_second)
     clear()
-    loop(tiles - 1, obs_wait)
+    obs_wait()
     for g in range(chunks):
         hot(g)
-    rs_wait(0)
+    rs_mid(0)
+    span(q1 + 1, q2, send_second)
     observe(0)
-    loop(members, functools.partial(forward, 1))
+    span(q2, q2 + 1, send_second)
+    span(0, q1, functools.partial(forward, 1))
+    ag_mid(0)
+    span(q2 + 1, members, send_second)
+    span(q1, q2, functools.partial(forward, 1))
+    ag_wait(0)
+    span(0, q1, functools.partial(force, 0))
+    span(q2, members, functools.partial(forward, 1))
     rs_start(1)
-    ag_wait(0)
-    loop(members, functools.partial(force, 0))
-    rs_wait(1)
+    span(q1, q1 + 1, functools.partial(force, 0))
+    rs_mid(1)
+    span(q1 + 1, q2, functools.partial(force, 0))
     observe(1)
-    loop(ens - 1, lambda k: dg_copy(k + 1).start())
+    dx_copy.start()
+    span(q2, q2 + 1, functools.partial(force, 0))
+    ag_mid(1)
+    dg_mid()
+    span(q2 + 1, members, functools.partial(force, 0))
     early = members // 4
     loop(early, backward_first)
     ag_wait(1)
@@ -656,29 +774,42 @@
     for copy in wind:
         copy.start()
 
-    loop(members, functools.partial(force, 1))
-
-    def dg_wait(k):
-        s = peer_e(k + 1)
-        remote(depp, dbuf.at[s], s_dg.at[s], r_dg.at[s], s, t).wait_recv()
-
-    loop(ens - 1, dg_wait)
-    dbuf[e] = depp[...]
-
-    def gather_dep(s):
-        value = dbuf[0, s]
-        for b in range(1, ens):
-            value = value + dbuf[b, s]
-        deps[s] = value
-
-    loop(tiles, gather_dep)
-
-    def dep_copy(k):
-        s = peer_t(k)
-        return remote(deps.at[s], depr.at[t], s_dep.at[s], r_dep.at[t], e, s)
-
-    loop(tiles - 1, lambda k: dep_copy(k + 1).start())
-    depr[t] = deps[t]
+    span(0, q1, functools.partial(force, 1))
+
+    each_y(
+        lambda b: remote(
+            depx, dbuf.at[b], s_dg.at[b], r_dg.at[b], 2 * b + xl, t
+        ).wait_recv()
+    )
+    dbuf[y] = depx[...]
+    value = dbuf[0]
+    for b in range(1, ny):
+        value = value + dbuf[b]
+    deps[...] = value
+
+    def dep_copy(j, s):
+        return remote(
+            deps.at[y, j], depr.at[y, line_t], s_dep.at[j], r_dep.at[line_t], e, s
+        )
+
+    each_kin(lambda j, s: dep_copy(j, s).start())
+
+    @pl.when(alone == 1)
+    def _():
+        depr[y, line_t] = deps[y, line_t]
+
+    span(q1, q2, functools.partial(force, 1))
+    each_kin(
+        lambda j, s: remote(
+            deps.at[y, j], depr.at[y, j], s_dep.at[j], r_dep.at[j], e, s
+        ).wait_recv()
+    )
+
+    def dep_on(b):
+        return remote(depr.at[y], depr.at[y], s_d2.at[b], r_d2.at[y], 2 * b + xl, t)
+
+    each_y(lambda b: dep_on(b).start())
+    span(q2, members, functools.partial(force, 1))
 
     for copy in wind:
         copy.wait_recv()
@@ -707,15 +838,18 @@
             ed[m, r] = pltpu.roll(pk_d[r], by, 1)
     loop(members, backward_second)
 
-    def dep_wait(k):
-        s = peer_t(k + 1)
-        remote(deps.at[s], depr.at[s], s_dep.at[s], r_dep.at[s], e, s).wait_recv()
-
-    loop(tiles - 1, dep_wait)
+    each_y(
+        lambda b: remote(
+            depr.at[b], depr.at[b], s_d2.at[b], r_d2.at[b], 2 * b + xl, t
+        ).wait_recv()
+    )
+    for d in range(tiles):
+        depf[d : d + 1, :] = depr[lax.rem(t + d, ny), d // ny]
+    lane, shift, usable = places(start_col, count_col)
     line_row = jnp.broadcast_to(start_row, (tiles, tiles)).astype(jnp.int32) // LANES
     spread0 = jnp.where(d_sub == line_row, 1.0, 0.0).astype(BF16)
     spread1 = jnp.where(d_sub == line_row + 1, 1.0, 0.0).astype(BF16)
-    value = turn(jnp.where(usable, depr[:, 0, :], 0.0), False)
+    value = turn(jnp.where(usable, depf[...], 0.0), shift, False)
     out = jnp.zeros((tiles, LANES), F32)
     for piece in split3(jnp.where(lane >= shift, value, 0.0)):
         out = out + jnp.dot(spread0, piece, preferred_element_type=F32)
@@ -736,19 +870,22 @@
 
     loop(members, sent)
 
-    def sent_t(k):
-        obs_copy(k + 1).wait_send()
-        dep_copy(k + 1).wait_send()
-
-    loop(tiles - 1, sent_t)
-
-    def sent_e(k):
+    each_kin(lambda j, d: obs_copy(j, d).wait_send())
+    each_kin(lambda j, d: dep_copy(j, d).wait_send())
+    dx_copy.wait_send()
+    for part in range(2):
+        rx_copy(part).wait_send()
+        ax_copy(part).wait_send()
+
+    def sent_y(b):
+        obs_on(b).wait_send()
+        dep_on(b).wait_send()
+        dg_copy(b).wait_send()
         for part in range(2):
-            rs_copy(part, k + 1).wait_send()
-            ag_copy(part, k + 1).wait_send()
-        dg_copy(k + 1).wait_send()
-
-    loop(ens - 1, sent_e)
+            rs_copy(part, b).wait_send()
+            ag_copy(part, b).wait_send()
+
+    each_y(sent_y)
 
 
 def hand_over(x0, x1, x2, y0, y1, y2, b0, b1, b2, s_in, s_out):
@@ -795,10 +932,13 @@
     wide = width + LANES
     band = width // 2 + 2 * LANES
     units = 2 * rows + 1
-    chunks = max(1, tiles // ens)
-    slots = min(ens, tiles) * LANES
+    ny = ens // 2
+    group = tiles // ny
+    chunks = ny
+    slots = group * LANES
     total_rows = rows + 2 * NDIFF
     fields = (members, rows) + line
+    halves = (members, 2, rows, lev, width // 2)
     scratch = [
         vmem(*ens_control.shape),
         vmem(*perturbations.shape, dtype=BF16),
@@ -820,20 +960,22 @@
         vmem(*line),
         vmem(*line),
         vmem(*line),
-        vmem(*fields),
-        vmem(*fields),
-        vmem(*fields),
+        vmem(*halves),
+        vmem(*halves),
+        vmem(*halves),
         vmem(NT, *fields),
-        vmem(*fields),
-        vmem(*fields),
-        vmem(*fields),
+        vmem(*halves),
+        vmem(*halves),
+        vmem(*halves),
         vmem(total_rows, lev, band),
         vmem(total_rows, lev, band),
         vmem(hi_n, lev, band),
         vmem(ens, units, lev, LANES),
-        vmem(ens, units, lev, LANES),
-        vmem(tiles, 2 * lev, LANES),
-        vmem(tiles, 2 * lev, LANES),
+        vmem(ny, 2, units, lev, LANES),
+        vmem(units, lev, LANES),
+        vmem(units, lev, LANES),
+        vmem(group, 2 * lev, LANES),
+        vmem(ny, group, 2 * lev, LANES),
         vmem(chunks, LANES, slots, dtype=BF16),
         vmem(chunks, lev, slots, dtype=jnp.int32),
         vmem(chunks, lev, slots),
@@ -847,20 +989,28 @@
         vmem(units, lev, LANES),
         vmem(ens, units, lev, LANES),
         vmem(hi_n, *line),
-        vmem(tiles, 1, LANES),
-        vmem(ens, tiles, 1, LANES),
-        vmem(tiles, 1, LANES),
-        vmem(tiles, 1, LANES),
+        vmem(ny, group, 1, LANES),
+        vmem(ny, group, 1, LANES),
+        vmem(ny, group, 1, LANES),
+        vmem(ny, ny, group, 1, LANES),
+        vmem(ny, group, 1, LANES),
+        vmem(ny, group, 1, LANES),
+        vmem(tiles, LANES),
         dma(4), dma(4),
         dma(2, 2, members), dma(2, 2, members),
         dma(2, 2, members), dma(2, 2, members),
-        dma(tiles), dma(tiles),
-        dma(2, ens), dma(2, ens),
-        dma(2, ens), dma(2, ens),
-        dma(ens), dma(ens),
+        dma(group), dma(group),
+        dma(2, ny), dma(2, ny),
+        dma(2, ny), dma(2, ny),
+        dma(ny), dma(ny),
         dma(2), dma(2),
-        dma(tiles), dma(tiles),
+        dma(group), dma(group),
         dma(2), dma(2),
+        dma(ny), dma(ny),
+        dma(2), dma(2),
+        dma(2), dma(2),
+        dma(1), dma(1),
+        dma(ny), dma(ny),
     ]
     v = pl.BlockSpec(memory_space=pltpu.VMEM)
     s = pl.BlockSpec(memory_space=pltpu.SMEM)

time: 90.2 us -> 89.1 us (0.988)
  Pallas kernels: 89.4 us -> 88.3 us
    pallas_call x1, Pallas kernels: 87.3 us -> 86.2 us  [per_device(): pl.pallas_call(functools.partial(kernel, factor, ens, tiles), out_shape=(...]
where the time goes in v5:
time: 89.1 us; the launch traced here: 89 us
  Pallas kernels  88.3 us (99%)
    pallas_call x1, Pallas kernels, per_device(): pl.pallas_call(functools.partial(kernel, factor, ens, tiles), out_shape=(...  86.2 us
    pallas_call x1, Pallas kernels, per_device(): pl.pallas_call(hand_over, out_shape=tuple((shape(x.shape, F32) for x in (...  2.17 us

profile of v5, /device:TPU:1, one launch (start us, length us, event | category | flops | bytes accessed | tf_op | source)
XLA Modules:
  0.0 89.0 jit_solution(323482241045434296)
XLA Ops:
  0.6 86.2 %gradient.1 = (f32[8,8,4,1024]{3,2,1,0:T(4,128)}, f32[8,4,1024]{2,1,0:T(4,128)}, f32[32,128]{1,0:T(8,128)}) custom-call(f32[8,8,4,1024]{3,2,1,0:T(4,128)} %ctl_hbm.1, f32[8,4,1024]{2,1,0:T(4,128)} %stc.1, bf16[2,8,8,4,1024]{4,3,2,1,0:T(4,128)(2,1)} %per_hbm.1, f32[8]{0:T(128)} %sigma.1, s32[4,1024]{1,0:T(4,128)} %cls.1, f32[4,1024]{1,0:T(4,128)} %east.1, ...), custom_call_target="tpu_custom_call" | custom-call | tf_op jit(solution)/shard_map/gradient/pallas_call | solution.py:1019
  86.8 2.2 %results.1 = (f32[8,8,4,1024]{3,2,1,0:T(4,128)}, f32[8,4,1024]{2,1,0:T(4,128)}, f32[32,128]{1,0:T(8,128)}) custom-call(f32[8,8,4,1024]{3,2,1,0:T(4,128)} %get-tuple-element.9.x0, f32[8,4,1024]{2,1,0:T(4,128)} %get-tuple-element.10.x1, f32[32,128]{1,0:T(8,128)} %get-tuple-element.11.x2), custom_call_target="tpu_custom_call" | custom-call | tf_op jit(solution)/shard_map/results/pallas_call | solution.py:1047

commit v6 on v5

v6 whole, which is shorter than its diff:
```python
import functools
import math

import jax
import jax.numpy as jnp
from jax import lax
from jax.experimental import pallas as pl
from jax.experimental.pallas import tpu as pltpu
from jax.sharding import PartitionSpec as P

NT = 2
NDIFF = 4
BETA_ENS = 0.8
BETA_STATIC = 0.6
DIFF_BASE = 0.06
LANES = 128
MESH = pl.DeviceIdType.MESH
F32 = jnp.float32
BF16 = jnp.bfloat16


def split3(x):
    a = x.astype(BF16)
    rest = x - a.astype(F32)
    b = rest.astype(BF16)
    c = (rest - b.astype(F32)).astype(BF16)
    return a, b, c


def split2(x):
    a = x.astype(BF16).astype(F32)
    return a, x - a


def left(x):
    return pltpu.roll(x, 1, 1)


def right(x):
    return pltpu.roll(x, x.shape[1] - 1, 1)


def kernel(
    factor,
    ens,
    tiles,
    ctl_hbm,
    stc,
    per_hbm,
    sigma,
    cls,
    east,
    north,
    ocol,
    ocnt,
    oval,
    owgt,
    oker,
    gens_hbm,
    gsta,
    gdep,
    ctl,
    per,
    gens,
    s_in,
    s_out,
    okb,
    dif,
    dif_u,
    dif_d,
    dbc,
    dsq,
    fin,
    sta,
    sta_u,
    sta_d,
    stb,
    wnd_u,
    wnd_d,
    rcv_wu,
    rcv_wd,
    cc,
    cu,
    cd,
    pp,
    ff,
    fu,
    fd,
    wa,
    wb,
    acc,
    accb,
    rbuf,
    obs_s,
    obs_r,
    onehot,
    himask,
    okern,
    oaux,
    adjb,
    abuf,
    adjf,
    depp,
    depx,
    dx,
    dbuf,
    deps,
    depr,
    depf,
    s_pre,
    r_pre,
    s_c,
    r_c,
    s_f,
    r_f,
    s_obs,
    r_obs,
    s_rs,
    r_rs,
    s_ag,
    r_ag,
    s_dg,
    r_dg,
    s_w,
    r_w,
    s_dep,
    r_dep,
    s_o2,
    r_o2,
    s_dx,
    r_dx,
    s_d2,
    r_d2,
):
    members, lev, rows, width = ctl.shape
    load_ctl = pltpu.make_async_copy(ctl_hbm, ctl, s_in.at[0])
    load_per = pltpu.make_async_copy(per_hbm, per, s_in.at[1])
    load_ctl.start()
    load_per.start()
    hi_n = NT * rows
    e = lax.axis_index("ens")
    t = lax.axis_index("tile")
    ny = ens // 2
    y = e // 2
    xl = lax.rem(e, 2)
    partner = 2 * y + 1 - xl
    group = tiles // ny
    kin = lax.rem(y - lax.rem(t, ny) + ny, ny)
    line_t = t // ny
    up = lax.rem(t + tiles - 1, tiles)
    down = lax.rem(t + 1, tiles)
    first = t == 0
    last = t == tiles - 1

    def remote(src, dst, ssem, rsem, e_to, t_to):
        return pltpu.make_async_remote_copy(
            src_ref=src,
            dst_ref=dst,
            send_sem=ssem,
            recv_sem=rsem,
            device_id=(e_to, t_to),
            device_id_type=MESH,
        )

    def loop(n, body):
        def step(i, carry):
            body(i)
            return carry

        lax.fori_loop(0, n, step, 0)

    def span(low, high, body):
        def step(i, carry):
            body(i)
            return carry

        lax.fori_loop(low, high, step, 0)

    def each_e(body):
        span(1, ens, lambda k: body(lax.rem(e + k, ens)))

    def peer_y(k):
        return lax.rem(y + k, ny)

    def each_y(body):
        span(1, ny, lambda k: body(peer_y(k)))

    def each_kin(body):
        def one(j):
            pl.when(j * ny + kin != t)(lambda: body(j, j * ny + kin))

        loop(group, one)

    barrier = pltpu.get_barrier_semaphore()

    def greet(e_to, t_to):
        pl.semaphore_signal(barrier, inc=1, device_id=(e_to, t_to), device_id_type=MESH)

    greet(e, up)
    greet(e, down)
    each_kin(lambda j, d: greet(e, d))
    each_e(lambda b: greet(b, t))
    alone = jnp.where(kin == lax.rem(t, ny), 1, 0)
    dif[...] = jnp.sqrt(DIFF_BASE * (cls[...].astype(F32) + 1.0))
    sub = lax.broadcasted_iota(jnp.int32, (lev, width), 0)
    scale = jnp.zeros((lev, width), F32)
    for l in range(lev):
        scale = jnp.where(sub == l, BETA_STATIC * sigma[l], scale)
    for r in range(rows):
        sta[r] = scale * stc[:, r, :]
    load_ctl.wait()
    pl.semaphore_wait(barrier, 2 + group - alone + ens - 1)

    pre = [
        remote(dif, dif_u, s_pre.at[0], r_pre.at[0], e, down),
        remote(dif, dif_d, s_pre.at[1], r_pre.at[1], e, up),
        remote(sta.at[rows - 1], sta_u, s_pre.at[2], r_pre.at[2], e, down),
        remote(sta.at[0], sta_d, s_pre.at[3], r_pre.at[3], e, up),
    ]
    for copy in pre:
        copy.start()

    def halo(m, own, from_up, from_down, ssem, rsem):
        src = own.at[m]
        return (
            remote(src, from_up.at[m], ssem.at[0, m], rsem.at[0, m], e, down),
            remote(src, from_down.at[m], ssem.at[1, m], rsem.at[1, m], e, up),
        )

    def send_control(m):
        for r in range(rows):
            cc[m, r] = ctl[m, :, r, :]
        for copy in halo(m, cc, cu, cd, s_c, r_c):
            copy.start()

    ahead = members // 4
    span(0, ahead, send_control)

    count = jnp.broadcast_to(ocnt[...].astype(F32), (tiles, tiles))
    d_sub = lax.broadcasted_iota(jnp.int32, (tiles, tiles), 0)
    d_lane = lax.broadcasted_iota(jnp.int32, (tiles, tiles), 1)
    count_col = jnp.sum(
        jnp.where(d_lane == d_sub, count, 0.0), axis=1, keepdims=True
    )
    start_col = jnp.sum(jnp.where(d_lane < d_sub, count, 0.0), axis=1, keepdims=True)
    start_row = jnp.sum(
        jnp.where(d_sub < d_lane, jnp.broadcast_to(count_col, (tiles, tiles)), 0.0),
        axis=0,
        keepdims=True,
    )
    def places(start_of, count_of):
        shape = (start_of.shape[0], LANES)
        begin = jnp.broadcast_to(start_of, shape).astype(jnp.int32)
        lane = lax.broadcasted_iota(jnp.int32, shape, 1)
        usable = lane < jnp.broadcast_to(count_of, shape).astype(jnp.int32)
        return lane, begin & (LANES - 1), usable

    def turn(x, shift, back):
        for bit in range(LANES.bit_length() - 1):
            by = LANES - (1 << bit) if back else 1 << bit
            x = jnp.where(shift & (1 << bit) != 0, pltpu.roll(x, by, 1), x)
        return x

    kin_count = jnp.broadcast_to(ocnt[...].astype(F32), (group, tiles))
    kin_sub = lax.broadcasted_iota(jnp.int32, (group, tiles), 0) * ny + kin
    kin_lane = lax.broadcasted_iota(jnp.int32, (group, tiles), 1)
    kin_start = jnp.sum(
        jnp.where(kin_lane < kin_sub, kin_count, 0.0), axis=1, keepdims=True
    )
    kin_own = jnp.sum(
        jnp.where(kin_lane == kin_sub, kin_count, 0.0), axis=1, keepdims=True
    )
    lane, shift, usable = places(kin_start, kin_own)
    line_col = jnp.broadcast_to(kin_start, (group, tiles)).astype(jnp.int32) // LANES
    pick = jnp.concatenate(
        [
            jnp.where(kin_lane == line_col, 1.0, 0.0),
            jnp.where(kin_lane == line_col + 1, 1.0, 0.0),
        ],
        axis=0,
    ).astype(BF16)
    for b in range(tiles):
        okb[b] = oker[:, b * LANES : (b + 1) * LANES]
    for q in range(lev + 3):
        if q < lev:
            part = okb[:, q, :]
        else:
            part = (ocol, oval, owgt)[q - lev][...].astype(F32)
        two = sum(
            jnp.dot(pick, piece, preferred_element_type=F32) for piece in split3(part)
        )
        value = jnp.where(lane >= shift, two[0:group], two[group : 2 * group])
        value = turn(value, shift, True)
        if q == lev:
            value = jnp.where(usable, value, -1.0)
        obs_s[:, q, :] = value
    for q in range(lev + 3, 2 * lev):
        obs_s[:, q, :] = jnp.zeros((group, LANES), F32)

    def obs_copy(j, d):
        return remote(
            obs_s.at[j], obs_r.at[y, line_t], s_obs.at[j], r_obs.at[line_t], e, d
        )

    each_kin(lambda j, d: obs_copy(j, d).start())

    @pl.when(alone == 1)
    def _():
        obs_r[y, line_t] = obs_s[line_t]

    span(ahead, members, send_control)

    def obs_on(b):
        return remote(obs_r.at[y], obs_r.at[y], s_o2.at[b], r_o2.at[y], 2 * b + xl, t)

    def obs_mid():
        each_kin(
            lambda j, d: remote(
                obs_s.at[j], obs_r.at[y, j], s_obs.at[j], r_obs.at[j], e, d
            ).wait_recv()
        )
        each_y(lambda b: obs_on(b).start())

    def obs_wait():
        each_y(
            lambda b: remote(
                obs_r.at[b], obs_r.at[b], s_o2.at[b], r_o2.at[b], 2 * b + xl, t
            ).wait_recv()
        )

    def spread(m):
        for s in range(NT):
            block = per[s, m].astype(F32)
            for r in range(rows):
                pp[s, m, r] = block[:, r, :]

    load_per.wait()
    loop(members, spread)

    pre[0].wait_recv()
    pre[1].wait_recv()
    above = jnp.where(first, 0.0, dif_u[...])
    below = jnp.where(last, 0.0, dif_d[...])
    own = dif[...]
    total_rows = rows + 2 * NDIFF
    for i in range(total_rows):
        src = above if i < NDIFF else (own if i < NDIFF + rows else below)
        j = i if i < NDIFF else (i - NDIFF if i < NDIFF + rows else i - NDIFF - rows)
        line = jnp.broadcast_to(src[j : j + 1, :], (lev, width))
        dbc[i] = line
        dsq[i] = line * line
        if NDIFF <= i < NDIFF + rows:
            fin[i - NDIFF] = factor / line

    def tile_of(x, b):
        return x[:, b * LANES : (b + 1) * LANES]

    pre[2].wait_recv()
    pre[3].wait_recv()

    def winds(r):
        we = jnp.broadcast_to(east[r : r + 1, :], (lev, width))
        wn = jnp.broadcast_to(north[r : r + 1, :], (lev, width))
        return (
            jnp.maximum(we, 0.0),
            jnp.minimum(we, 0.0),
            jnp.maximum(wn, 0.0),
            jnp.minimum(wn, 0.0),
        )

    for r in range(rows):
        ep, em, np_, nm = winds(r)
        q = sta[r]
        above = sta[r - 1] if r else jnp.where(first, 0.0, sta_u[...])
        below = sta[r + 1] if r < rows - 1 else jnp.where(last, 0.0, sta_d[...])
        moved = q - ep * (q - left(q)) - em * (right(q) - q)
        moved = moved - np_ * (q - above) - nm * (below - q)
        for b in range(ens):
            stb[b, r] = tile_of(q, b)
            stb[b, rows + r] = tile_of(moved, b)

    def smooth(m, refs):
        for i in range(total_rows):
            ref, r = source_of(i, refs)
            wa[i] = dbc[i] * ref[m, r]
        src, dst = wa, wb
        for step in range(NDIFF):
            for i in range(step + 1, total_rows - 1 - step):
                w = src[i]
                lap = src[i + 1] + src[i - 1] + left(w) + right(w) - 4.0 * w
                dst[i] = w + dsq[i] * lap
            src, dst = dst, src
        return [src[NDIFF + r] for r in range(rows)]

    def source_of(i, refs):
        if i < NDIFF:
            return refs[0], i
        if i < NDIFF + rows:
            return refs[1], i - NDIFF
        return refs[2], i - NDIFF - rows

    def forward(m):
        for copy in halo(m, cc, cu, cd, s_c, r_c):
            copy.wait_recv()
        res = smooth(m, (cu, cc, cd))
        for r in range(rows):
            for s in range(NT):
                acc[s * rows + r] += pp[s, m, r] * res[r]

    def rs_copy(b):
        return remote(accb.at[b], rbuf.at[e], s_rs.at[b], r_rs.at[e], b, t)

    def rs_start():
        for h in range(hi_n):
            value = acc[h] * fin[h % rows]
            for b in range(ens):
                accb[b, h] = tile_of(value, b)
        each_e(lambda b: rs_copy(b).start())

    def rs_wait():
        each_e(
            lambda b: remote(
                accb.at[b], rbuf.at[b], s_rs.at[b], r_rs.at[b], b, t
            ).wait_recv()
        )
        rbuf[e] = accb[e]

    chunks = ny

    def lines_of(g, i, n=1):
        return jnp.concatenate(
            [obs_r[g, j, i : i + n, :] for j in range(group)], axis=1
        )

    lo_iota = lax.broadcasted_iota(jnp.int32, (LANES, group * LANES), 0)

    def hot(g):
        col = lines_of(g, lev).astype(jnp.int32)
        lo = col & (LANES - 1)
        block = (col // LANES) & (ens - 1)
        unit = jnp.where((col >= 0) & (block == e), col // width, -1)
        himask[g] = jnp.broadcast_to(unit, (lev, group * LANES))
        okern[g] = lines_of(g, 0, lev)
        oaux[g, 0:1, :] = lines_of(g, lev + 1)
        oaux[g, 1:2, :] = lines_of(g, lev + 2)
        onehot[g] = jnp.where(
            jnp.broadcast_to(lo, (LANES, group * LANES)) == lo_iota, 1.0, 0.0
        ).astype(BF16)

    def observe():
        points = hi_n * lev
        values = []
        for u in range(hi_n):
            value = stb[e, u]
            for b in range(ens):
                value = value + rbuf[b, u]
            values.append(value)
        table = jnp.concatenate(split2(jnp.concatenate(values, axis=0)), axis=0)
        table = table.astype(BF16)
        total = jnp.zeros((2 * points, LANES), F32)
        for g in range(chunks):
            hi = himask[g]
            kern = okern[g]
            flat = jnp.dot(table, onehot[g], preferred_element_type=F32)
            profile = jnp.zeros(kern.shape, F32)
            for j in range(hi_n):
                value = flat[j * lev : (j + 1) * lev]
                value = value + flat[points + j * lev : points + (j + 1) * lev]
                profile = jnp.where(hi == j, value, profile)
            evolved = jnp.sum(kern * profile, axis=0, keepdims=True)
            dep = oaux[g, 1:2, :] * (evolved - oaux[g, 0:1, :])
            dep = jnp.where(hi[0:1] >= 0, dep, 0.0)
            for j in range(group):
                depp[g, j] = tile_of(dep, j)
            push = kern * dep
            place = jnp.concatenate(
                [jnp.where(hi == j, push, 0.0) for j in range(hi_n)], axis=0
            )
            place = jnp.concatenate(split2(place), axis=0).astype(BF16)
            total = total + lax.dot_general(
                place, onehot[g], (((1,), (1,)), ((), ())), preferred_element_type=F32
            )
        total = total[0:points] + total[points : 2 * points]
        for j in range(hi_n):
            adjb[j] = total[j * lev : (j + 1) * lev]
            abuf[e, j] = total[j * lev : (j + 1) * lev]
        each_e(lambda b: ag_copy(b).start())

    def ag_copy(b):
        return remote(adjb, abuf.at[e], s_ag.at[b], r_ag.at[e], b, t)

    def ag_wait():
        each_e(
            lambda b: remote(
                adjb, abuf.at[b], s_ag.at[b], r_ag.at[b], b, t
            ).wait_recv()
        )
        for h in range(hi_n):
            adjf[h] = jnp.concatenate([abuf[b, h] for b in range(ens)], axis=1)

    dx_copy = remote(depp, dx, s_dx.at[0], r_dx.at[0], partner, t)

    def dg_copy(b):
        return remote(depx, dbuf.at[y], s_dg.at[b], r_dg.at[y], 2 * b + xl, t)

    def dg_mid():
        dx_copy.wait_recv()
        depx[...] = depp[...] + dx[...]
        each_y(lambda b: dg_copy(b).start())

    def force(m):
        for r in range(rows):
            ff[m, r] = pp[0, m, r] * adjf[r] + pp[1, m, r] * adjf[rows + r]
        for copy in halo(m, ff, fu, fd, s_f, r_f):
            copy.start()

    def store_of(m):
        return pltpu.make_async_copy(gens.at[m], gens_hbm.at[m], s_out.at[m])

    def backward(m):
        for copy in halo(m, ff, fu, fd, s_f, r_f):
            copy.wait_recv()
        res = smooth(m, (fu, ff, fd))
        for r in range(rows):
            gens[m, :, r, :] = cc[m, r] + res[r] * fin[r]
        store_of(m).start()

    for h in range(hi_n):
        acc[h] = jnp.zeros((lev, width), F32)
    span(0, members // 2, forward)
    obs_mid()
    span(members // 2, members, forward)
    rs_start()
    obs_wait()
    for g in range(chunks):
        hot(g)
    rs_wait()
    observe()
    dx_copy.start()
    ag_wait()
    wnd_u[...] = winds(0)[2] * adjf[rows]
    wnd_d[...] = winds(rows - 1)[3] * adjf[2 * rows - 1]
    wind = [
        remote(wnd_d, rcv_wu, s_w.at[0], r_w.at[0], e, down),
        remote(wnd_u, rcv_wd, s_w.at[1], r_w.at[1], e, up),
    ]
    q1, q2 = members // 4, members * 5 // 8
    span(0, 1, force)
    for copy in wind:
        copy.start()
    dg_mid()
    span(1, q1, force)

    each_y(
        lambda b: remote(
            depx, dbuf.at[b], s_dg.at[b], r_dg.at[b], 2 * b + xl, t
        ).wait_recv()
    )
    dbuf[y] = depx[...]
    value = dbuf[0]
    for b in range(1, ny):
        value = value + dbuf[b]
    deps[...] = value

    def dep_copy(j, s):
        return remote(
            deps.at[y, j], depr.at[y, line_t], s_dep.at[j], r_dep.at[line_t], e, s
        )

    each_kin(lambda j, s: dep_copy(j, s).start())

    @pl.when(alone == 1)
    def _():
        depr[y, line_t] = deps[y, line_t]

    span(q1, q2, force)
    each_kin(
        lambda j, s: remote(
            deps.at[y, j], depr.at[y, j], s_dep.at[j], r_dep.at[j], e, s
        ).wait_recv()
    )

    def dep_on(b):
        return remote(depr.at[y], depr.at[y], s_d2.at[b], r_d2.at[y], 2 * b + xl, t)

    each_y(lambda b: dep_on(b).start())
    span(q2, members, force)

    for copy in wind:
        copy.wait_recv()
    for r in range(rows):
        ep, em, np_, nm = winds(r)
        a = adjf[rows + r]
        if r < rows - 1:
            lower = winds(r + 1)[2] * adjf[rows + r + 1]
        else:
            lower = jnp.where(last, 0.0, rcv_wd[...])
        if r:
            upper = winds(r - 1)[3] * adjf[rows + r - 1]
        else:
            upper = jnp.where(first, 0.0, rcv_wu[...])
        moved = a * (1.0 - ep + em - np_ + nm) + right(ep * a) - left(em * a)
        moved = moved + lower - upper
        gsta[:, r, :] = stc[:, r, :] + scale * (adjf[r] + moved)

    span(0, q2, backward)

    each_y(
        lambda b: remote(
            depr.at[b], depr.at[b], s_d2.at[b], r_d2.at[b], 2 * b + xl, t
        ).wait_recv()
    )
    for d in range(tiles):
        depf[d : d + 1, :] = depr[lax.rem(t + d, ny), d // ny]
    lane, shift, usable = places(start_col, count_col)
    line_row = jnp.broadcast_to(start_row, (tiles, tiles)).astype(jnp.int32) // LANES
    spread0 = jnp.where(d_sub == line_row, 1.0, 0.0).astype(BF16)
    spread1 = jnp.where(d_sub == line_row + 1, 1.0, 0.0).astype(BF16)
    value = turn(jnp.where(usable, depf[...], 0.0), shift, False)
    out = jnp.zeros((tiles, LANES), F32)
    for piece in split3(jnp.where(lane >= shift, value, 0.0)):
        out = out + jnp.dot(spread0, piece, preferred_element_type=F32)
    for piece in split3(jnp.where(lane < shift, value, 0.0)):
        out = out + jnp.dot(spread1, piece, preferred_element_type=F32)
    gdep[...] = out
    span(q2, members, backward)

    loop(members, lambda m: store_of(m).wait())
    for copy in pre + wind:
        copy.wait_send()

    def sent(m):
        for copy in halo(m, cc, cu, cd, s_c, r_c) + halo(m, ff, fu, fd, s_f, r_f):
            copy.wait_send()

    loop(members, sent)

    each_kin(lambda j, d: obs_copy(j, d).wait_send())
    each_kin(lambda j, d: dep_copy(j, d).wait_send())
    dx_copy.wait_send()
    def sent_y(b):
        obs_on(b).wait_send()
        dep_on(b).wait_send()
        dg_copy(b).wait_send()

    each_y(sent_y)
    each_e(lambda b: rs_copy(b).wait_send())
    each_e(lambda b: ag_copy(b).wait_send())


def hand_over(x0, x1, x2, y0, y1, y2, b0, b1, b2, s_in, s_out):
    members = x0.shape[0]
    triples = [(x0.at[m], b0.at[m], y0.at[m]) for m in range(members)]
    triples += [(x1, b1, y1), (x2, b2, y2)]
    come = [
        pltpu.make_async_copy(x, b, s_in.at[i]) for i, (x, b, y) in enumerate(triples)
    ]
    go = [
        pltpu.make_async_copy(b, y, s_out.at[i]) for i, (x, b, y) in enumerate(triples)
    ]
    for copy in come:
        copy.start()
    for a, b in zip(come, go):
        a.wait()
        b.start()
    for copy in go:
        copy.wait()


def per_device(
    ens_control,
    static_control,
    perturbations,
    level_sigma,
    length_class,
    courant_east,
    courant_north,
    obs_column,
    obs_count,
    obs_value,
    obs_weight,
    obs_kernel,
):
    members, lev, rows, width = ens_control.shape
    ens = lax.axis_size("ens")
    tiles = lax.axis_size("tile")
    factor = BETA_ENS / math.sqrt(ens * members - 1)
    hi_n = NT * rows
    vmem = lambda *shape, dtype=F32: pltpu.VMEM(shape, dtype)
    dma = lambda *shape: pltpu.SemaphoreType.DMA(shape)
    line = (lev, width)
    ny = ens // 2
    group = tiles // ny
    chunks = ny
    slots = group * LANES
    total_rows = rows + 2 * NDIFF
    fields = (members, rows) + line
    scratch = [
        vmem(*ens_control.shape),
        vmem(*perturbations.shape, dtype=BF16),
        vmem(*ens_control.shape),
        dma(2),
        dma(members),
        vmem(tiles, lev, LANES),
        vmem(rows, width),
        vmem(rows, width),
        vmem(rows, width),
        vmem(total_rows, lev, width),
        vmem(total_rows, lev, width),
        vmem(rows, lev, width),
        vmem(rows, *line),
        vmem(*line),
        vmem(*line),
        vmem(ens, hi_n, lev, LANES),
        vmem(*line),
        vmem(*line),
        vmem(*line),
        vmem(*line),
        vmem(*fields),
        vmem(*fields),
        vmem(*fields),
        vmem(NT, *fields),
        vmem(*fields),
        vmem(*fields),
        vmem(*fields),
        vmem(total_rows, lev, width),
        vmem(total_rows, lev, width),
        vmem(hi_n, lev, width),
        vmem(ens, hi_n, lev, LANES),
        vmem(ens, hi_n, lev, LANES),
        vmem(group, 2 * lev, LANES),
        vmem(ny, group, 2 * lev, LANES),
        vmem(chunks, LANES, slots, dtype=BF16),
        vmem(chunks, lev, slots, dtype=jnp.int32),
        vmem(chunks, lev, slots),
        vmem(chunks, lev, slots),
        vmem(hi_n, lev, LANES),
        vmem(ens, hi_n, lev, LANES),
        vmem(hi_n, *line),
        vmem(ny, group, 1, LANES),
        vmem(ny, group, 1, LANES),
        vmem(ny, group, 1, LANES),
        vmem(ny, ny, group, 1, LANES),
        vmem(ny, group, 1, LANES),
        vmem(ny, group, 1, LANES),
        vmem(tiles, LANES),
        dma(4), dma(4),
        dma(2, members), dma(2, members),
        dma(2, members), dma(2, members),
        dma(group), dma(group),
        dma(ens), dma(ens),
        dma(ens), dma(ens),
        dma(ny), dma(ny),
        dma(2), dma(2),
        dma(group), dma(group),
        dma(ny), dma(ny),
        dma(1), dma(1),
        dma(ny), dma(ny),
    ]
    v = pl.BlockSpec(memory_space=pltpu.VMEM)
    s = pl.BlockSpec(memory_space=pltpu.SMEM)
    a = pl.BlockSpec(memory_space=pl.ANY)
    shape = jax.ShapeDtypeStruct
    grad_ens, grad_static, departures = pl.pallas_call(
        functools.partial(kernel, factor, ens, tiles),
        out_shape=(
            shape(ens_control.shape, F32),
            shape(static_control.shape, F32),
            shape((tiles, LANES), F32),
        ),
        in_specs=[a, v, a, s, v, v, v, v, v, v, v, v],
        out_specs=(a, v, v),
        scratch_shapes=scratch,
        name="gradient",
        compiler_params=pltpu.CompilerParams(
            collective_id=0, has_side_effects=True, vmem_limit_bytes=56 * 2**20
        ),
    )(
        ens_control,
        static_control,
        perturbations,
        level_sigma,
        length_class,
        courant_east,
        courant_north,
        obs_column.reshape(tiles, LANES),
        obs_count.reshape(1, tiles),
        obs_value.reshape(tiles, LANES),
        obs_weight.reshape(tiles, LANES),
        obs_kernel,
    )
    grad_ens, grad_static, departures = pl.pallas_call(
        hand_over,
        out_shape=tuple(shape(x.shape, F32) for x in (grad_ens, grad_static, departures)),
        in_specs=[a, a, a],
        out_specs=(a, a, a),
        scratch_shapes=[
            vmem(*x.shape) for x in (grad_ens, grad_static, departures)
        ]
        + [dma(members + 2), dma(members + 2)],
        name="results",
    )(grad_ens, grad_static, departures)
    return (grad_ens, grad_static, departures.reshape(-1))


def solution(mesh):
    return jax.shard_map(
        per_device,
        mesh=mesh,
        in_specs=(
            P("ens", None, "tile", None),
            P(None, "tile", None),
            P(None, "ens", None, "tile", None),
            P(),
            P("tile", None),
            P("tile", None),
            P("tile", None),
            P("tile"),
            P("tile"),
            P("tile"),
            P("tile"),
            P(None, "tile"),
        ),
        out_specs=(P("ens", None, "tile", None), P(None, "tile", None), P("tile")),
        check_vma=False,
    )
```

time: 89.1 us -> 87.4 us (0.981)
  Pallas kernels: 88.3 us -> 86.6 us
    pallas_call x1, Pallas kernels: 86.2 us -> 84.4 us  [per_device(): pl.pallas_call(functools.partial(kernel, factor, ens, tiles), out_shape=(...]
where the time goes in v6:
time: 87.4 us; the launch traced here: 87.2 us
  Pallas kernels  86.6 us (99%)
    pallas_call x1, Pallas kernels, per_device(): pl.pallas_call(functools.partial(kernel, factor, ens, tiles), out_shape=(...  84.4 us
    pallas_call x1, Pallas kernels, per_device(): pl.pallas_call(hand_over, out_shape=tuple((shape(x.shape, F32) for x in (...  2.17 us

profile of v6, /device:TPU:1, one launch (start us, length us, event | category | flops | bytes accessed | tf_op | source)
XLA Modules:
  0.0 87.2 jit_solution(3276352119549520919)
XLA Ops:
  0.6 84.4 %gradient.1 = (f32[8,8,4,1024]{3,2,1,0:T(4,128)}, f32[8,4,1024]{2,1,0:T(4,128)}, f32[32,128]{1,0:T(8,128)}) custom-call(f32[8,8,4,1024]{3,2,1,0:T(4,128)} %ctl_hbm.1, f32[8,4,1024]{2,1,0:T(4,128)} %stc.1, bf16[2,8,8,4,1024]{4,3,2,1,0:T(4,128)(2,1)} %per_hbm.1, f32[8]{0:T(128)} %sigma.1, s32[4,1024]{1,0:T(4,128)} %cls.1, f32[4,1024]{1,0:T(4,128)} %east.1, ...), custom_call_target="tpu_custom_call" | custom-call | tf_op jit(solution)/shard_map/gradient/pallas_call | solution.py:764
  85.1 2.2 %results.1 = (f32[8,8,4,1024]{3,2,1,0:T(4,128)}, f32[8,4,1024]{2,1,0:T(4,128)}, f32[32,128]{1,0:T(8,128)}) custom-call(f32[8,8,4,1024]{3,2,1,0:T(4,128)} %get-tuple-element.9.x0, f32[8,4,1024]{2,1,0:T(4,128)} %get-tuple-element.10.x1, f32[32,128]{1,0:T(8,128)} %get-tuple-element.11.x2), custom_call_target="tpu_custom_call" | custom-call | tf_op jit(solution)/shard_map/results/pallas_call | solution.py:792

commit v7 on v6

--- a/solution.py
+++ b/solution.py
@@ -544,12 +544,11 @@
         remote(wnd_d, rcv_wu, s_w.at[0], r_w.at[0], e, down),
         remote(wnd_u, rcv_wd, s_w.at[1], r_w.at[1], e, up),
     ]
-    q1, q2 = members // 4, members * 5 // 8
-    span(0, 1, force)
+    q1, q2 = members * 3 // 8, members * 3 // 4
+    dg_mid()
+    span(0, q1, force)
     for copy in wind:
         copy.start()
-    dg_mid()
-    span(1, q1, force)
 
     each_y(
         lambda b: remote(
@@ -574,17 +573,6 @@
         depr[y, line_t] = deps[y, line_t]
 
     span(q1, q2, force)
-    each_kin(
-        lambda j, s: remote(
-            deps.at[y, j], depr.at[y, j], s_dep.at[j], r_dep.at[j], e, s
-        ).wait_recv()
-    )
-
-    def dep_on(b):
-        return remote(depr.at[y], depr.at[y], s_d2.at[b], r_d2.at[y], 2 * b + xl, t)
-
-    each_y(lambda b: dep_on(b).start())
-    span(q2, members, force)
 
     for copy in wind:
         copy.wait_recv()
@@ -603,7 +591,19 @@
         moved = moved + lower - upper
         gsta[:, r, :] = stc[:, r, :] + scale * (adjf[r] + moved)
 
-    span(0, q2, backward)
+    span(0, q1, backward)
+    each_kin(
+        lambda j, s: remote(
+            deps.at[y, j], depr.at[y, j], s_dep.at[j], r_dep.at[j], e, s
+        ).wait_recv()
+    )
+
+    def dep_on(b):
+        return remote(depr.at[y], depr.at[y], s_d2.at[b], r_d2.at[y], 2 * b + xl, t)
+
+    each_y(lambda b: dep_on(b).start())
+    span(q2, members, force)
+    span(q1, members - 1, backward)
 
     each_y(
         lambda b: remote(
@@ -623,7 +623,7 @@
     for piece in split3(jnp.where(lane < shift, value, 0.0)):
         out = out + jnp.dot(spread1, piece, preferred_element_type=F32)
     gdep[...] = out
-    span(q2, members, backward)
+    span(members - 1, members, backward)
 
     loop(members, lambda m: store_of(m).wait())
     for copy in pre + wind:

time: 87.4 us -> 86.1 us (0.985)
  Pallas kernels: 86.6 us -> 85.3 us
    pallas_call x1, Pallas kernels: 84.4 us -> 83.2 us  [per_device(): pl.pallas_call(functools.partial(kernel, factor, ens, tiles), out_shape=(...]
where the time goes in v7:
time: 86.1 us; the launch traced here: 86 us
  Pallas kernels  85.3 us (99%)
    pallas_call x1, Pallas kernels, per_device(): pl.pallas_call(functools.partial(kernel, factor, ens, tiles), out_shape=(...  83.2 us
    pallas_call x1, Pallas kernels, per_device(): pl.pallas_call(hand_over, out_shape=tuple((shape(x.shape, F32) for x in (...  2.17 us

profile of v7, /device:TPU:1, one launch (start us, length us, event | category | flops | bytes accessed | tf_op | source)
XLA Modules:
  0.0 86.0 jit_solution(8124599844861588313)
XLA Ops:
  0.6 83.2 %gradient.1 = (f32[8,8,4,1024]{3,2,1,0:T(4,128)}, f32[8,4,1024]{2,1,0:T(4,128)}, f32[32,128]{1,0:T(8,128)}) custom-call(f32[8,8,4,1024]{3,2,1,0:T(4,128)} %ctl_hbm.1, f32[8,4,1024]{2,1,0:T(4,128)} %stc.1, bf16[2,8,8,4,1024]{4,3,2,1,0:T(4,128)(2,1)} %per_hbm.1, f32[8]{0:T(128)} %sigma.1, s32[4,1024]{1,0:T(4,128)} %cls.1, f32[4,1024]{1,0:T(4,128)} %east.1, ...), custom_call_target="tpu_custom_call" | custom-call | tf_op jit(solution)/shard_map/gradient/pallas_call | solution.py:764
  83.8 2.2 %results.1 = (f32[8,8,4,1024]{3,2,1,0:T(4,128)}, f32[8,4,1024]{2,1,0:T(4,128)}, f32[32,128]{1,0:T(8,128)}) custom-call(f32[8,8,4,1024]{3,2,1,0:T(4,128)} %get-tuple-element.9.x0, f32[8,4,1024]{2,1,0:T(4,128)} %get-tuple-element.10.x1, f32[32,128]{1,0:T(8,128)} %get-tuple-element.11.x2), custom_call_target="tpu_custom_call" | custom-call | tf_op jit(solution)/shard_map/results/pallas_call | solution.py:792

commit v8 on v7

--- a/solution.py
+++ b/solution.py
@@ -544,7 +544,7 @@
         remote(wnd_d, rcv_wu, s_w.at[0], r_w.at[0], e, down),
         remote(wnd_u, rcv_wd, s_w.at[1], r_w.at[1], e, up),
     ]
-    q1, q2 = members * 3 // 8, members * 3 // 4
+    q1 = members * 3 // 8
     dg_mid()
     span(0, q1, force)
     for copy in wind:
@@ -572,7 +572,7 @@
     def _():
         depr[y, line_t] = deps[y, line_t]
 
-    span(q1, q2, force)
+    span(q1, members, force)
 
     for copy in wind:
         copy.wait_recv()
@@ -602,8 +602,7 @@
         return remote(depr.at[y], depr.at[y], s_d2.at[b], r_d2.at[y], 2 * b + xl, t)
 
     each_y(lambda b: dep_on(b).start())
-    span(q2, members, force)
-    span(q1, members - 1, backward)
+    span(q1, members, backward)
 
     each_y(
         lambda b: remote(
@@ -623,7 +622,6 @@
     for piece in split3(jnp.where(lane < shift, value, 0.0)):
         out = out + jnp.dot(spread1, piece, preferred_element_type=F32)
     gdep[...] = out
-    span(members - 1, members, backward)
 
     loop(members, lambda m: store_of(m).wait())
     for copy in pre + wind:

time: 86.1 us -> 86.2 us (level)
  no operation moved by 1% of the time
where the time goes in v8:
time: 86.2 us; the launch traced here: 86.1 us
  Pallas kernels  85.4 us (99%)
    pallas_call x1, Pallas kernels, per_device(): pl.pallas_call(functools.partial(kernel, factor, ens, tiles), out_shape=(...  83.3 us
    pallas_call x1, Pallas kernels, per_device(): pl.pallas_call(hand_over, out_shape=tuple((shape(x.shape, F32) for x in (...  2.17 us

profile of v8, /device:TPU:1, one launch (start us, length us, event | category | flops | bytes accessed | tf_op | source)
XLA Modules:
  0.0 86.1 jit_solution(6717815961449231936)
XLA Ops:
  0.6 83.3 %gradient.1 = (f32[8,8,4,1024]{3,2,1,0:T(4,128)}, f32[8,4,1024]{2,1,0:T(4,128)}, f32[32,128]{1,0:T(8,128)}) custom-call(f32[8,8,4,1024]{3,2,1,0:T(4,128)} %ctl_hbm.1, f32[8,4,1024]{2,1,0:T(4,128)} %stc.1, bf16[2,8,8,4,1024]{4,3,2,1,0:T(4,128)(2,1)} %per_hbm.1, f32[8]{0:T(128)} %sigma.1, s32[4,1024]{1,0:T(4,128)} %cls.1, f32[4,1024]{1,0:T(4,128)} %east.1, ...), custom_call_target="tpu_custom_call" | custom-call | tf_op jit(solution)/shard_map/gradient/pallas_call | solution.py:762
  83.9 2.2 %results.1 = (f32[8,8,4,1024]{3,2,1,0:T(4,128)}, f32[8,4,1024]{2,1,0:T(4,128)}, f32[32,128]{1,0:T(8,128)}) custom-call(f32[8,8,4,1024]{3,2,1,0:T(4,128)} %get-tuple-element.9.x0, f32[8,4,1024]{2,1,0:T(4,128)} %get-tuple-element.10.x1, f32[32,128]{1,0:T(8,128)} %get-tuple-element.11.x2), custom_call_target="tpu_custom_call" | custom-call | tf_op jit(solution)/shard_map/results/pallas_call | solution.py:790

commit v9 on v8

--- a/solution.py
+++ b/solution.py
@@ -45,8 +45,23 @@
     ens,
     tiles,
     ctl_hbm,
+    stc_hbm,
+    per_hbm,
+    sigma_hbm,
+    cls_hbm,
+    east_hbm,
+    north_hbm,
+    ocol_hbm,
+    ocnt_hbm,
+    oval_hbm,
+    owgt_hbm,
+    oker_hbm,
+    gens_hbm,
+    gsta_hbm,
+    gdep,
+    ctl,
     stc,
-    per_hbm,
+    per,
     sigma,
     cls,
     east,
@@ -56,12 +71,8 @@
     oval,
     owgt,
     oker,
-    gens_hbm,
+    gens,
     gsta,
-    gdep,
-    ctl,
-    per,
-    gens,
     s_in,
     s_out,
     okb,
@@ -133,10 +144,6 @@
     r_d2,
 ):
     members, lev, rows, width = ctl.shape
-    load_ctl = pltpu.make_async_copy(ctl_hbm, ctl, s_in.at[0])
-    load_per = pltpu.make_async_copy(per_hbm, per, s_in.at[1])
-    load_ctl.start()
-    load_per.start()
     hi_n = NT * rows
     e = lax.axis_index("ens")
     t = lax.axis_index("tile")
@@ -201,6 +208,27 @@
     each_kin(lambda j, d: greet(e, d))
     each_e(lambda b: greet(b, t))
     alone = jnp.where(kin == lax.rem(t, ny), 1, 0)
+    inputs = (
+        (cls_hbm, cls),
+        (stc_hbm, stc),
+        (sigma_hbm, sigma),
+        (ctl_hbm, ctl),
+        (ocnt_hbm, ocnt),
+        (oker_hbm, oker),
+        (ocol_hbm, ocol),
+        (oval_hbm, oval),
+        (owgt_hbm, owgt),
+        (per_hbm, per),
+        (east_hbm, east),
+        (north_hbm, north),
+    )
+    loads = [
+        pltpu.make_async_copy(src, dst, s_in.at[i]) for i, (src, dst) in enumerate(inputs)
+    ]
+    for copy in loads:
+        copy.start()
+    for copy in loads[0:3]:
+        copy.wait()
     dif[...] = jnp.sqrt(DIFF_BASE * (cls[...].astype(F32) + 1.0))
     sub = lax.broadcasted_iota(jnp.int32, (lev, width), 0)
     scale = jnp.zeros((lev, width), F32)
@@ -208,7 +236,7 @@
         scale = jnp.where(sub == l, BETA_STATIC * sigma[l], scale)
     for r in range(rows):
         sta[r] = scale * stc[:, r, :]
-    load_ctl.wait()
+    loads[3].wait()
     pl.semaphore_wait(barrier, 2 + group - alone + ens - 1)
 
     pre = [
@@ -235,6 +263,9 @@
 
     ahead = members // 4
     span(0, ahead, send_control)
+
+    for copy in loads[4:9]:
+        copy.wait()
 
     count = jnp.broadcast_to(ocnt[...].astype(F32), (tiles, tiles))
     d_sub = lax.broadcasted_iota(jnp.int32, (tiles, tiles), 0)
@@ -334,7 +365,8 @@
             for r in range(rows):
                 pp[s, m, r] = block[:, r, :]
 
-    load_per.wait()
+    for copy in loads[9:12]:
+        copy.wait()
     loop(members, spread)
 
     pre[0].wait_recv()
@@ -545,8 +577,9 @@
         remote(wnd_u, rcv_wd, s_w.at[1], r_w.at[1], e, up),
     ]
     q1 = members * 3 // 8
+    span(0, 1, force)
     dg_mid()
-    span(0, q1, force)
+    span(1, q1, force)
     for copy in wind:
         copy.start()
 
@@ -591,6 +624,9 @@
         moved = moved + lower - upper
         gsta[:, r, :] = stc[:, r, :] + scale * (adjf[r] + moved)
 
+    store_static = pltpu.make_async_copy(gsta, gsta_hbm, s_out.at[members])
+    store_static.start()
+
     span(0, q1, backward)
     each_kin(
         lambda j, s: remote(
@@ -624,6 +660,7 @@
     gdep[...] = out
 
     loop(members, lambda m: store_of(m).wait())
+    store_static.wait()
     for copy in pre + wind:
         copy.wait_send()
 
@@ -695,10 +732,21 @@
     fields = (members, rows) + line
     scratch = [
         vmem(*ens_control.shape),
+        vmem(*static_control.shape),
         vmem(*perturbations.shape, dtype=BF16),
+        pltpu.SMEM(level_sigma.shape, F32),
+        vmem(*length_class.shape, dtype=jnp.int32),
+        vmem(*courant_east.shape),
+        vmem(*courant_north.shape),
+        vmem(tiles, LANES, dtype=jnp.int32),
+        vmem(1, tiles, dtype=jnp.int32),
+        vmem(tiles, LANES),
+        vmem(tiles, LANES),
+        vmem(*obs_kernel.shape),
         vmem(*ens_control.shape),
-        dma(2),
-        dma(members),
+        vmem(*static_control.shape),
+        dma(12),
+        dma(members + 1),
         vmem(tiles, lev, LANES),
         vmem(rows, width),
         vmem(rows, width),
@@ -756,7 +804,6 @@
         dma(ny), dma(ny),
     ]
     v = pl.BlockSpec(memory_space=pltpu.VMEM)
-    s = pl.BlockSpec(memory_space=pltpu.SMEM)
     a = pl.BlockSpec(memory_space=pl.ANY)
     shape = jax.ShapeDtypeStruct
     grad_ens, grad_static, departures = pl.pallas_call(
@@ -766,8 +813,8 @@
             shape(static_control.shape, F32),
             shape((tiles, LANES), F32),
         ),
-        in_specs=[a, v, a, s, v, v, v, v, v, v, v, v],
-        out_specs=(a, v, v),
+        in_specs=[a] * 12,
+        out_specs=(a, a, v),
         scratch_shapes=scratch,
         name="gradient",
         compiler_params=pltpu.CompilerParams(

time: 86.2 us -> 84.9 us (0.985)
  Pallas kernels: 85.4 us -> 84.1 us
    pallas_call x1, Pallas kernels: 83.3 us -> 82 us  [per_device(): pl.pallas_call(functools.partial(kernel, factor, ens, tiles), out_shape=(...]
where the time goes in v9:
time: 84.9 us; the launch traced here: 84.8 us
  Pallas kernels  84.1 us (99%)
    pallas_call x1, Pallas kernels, per_device(): pl.pallas_call(functools.partial(kernel, factor, ens, tiles), out_shape=(...  82 us
    pallas_call x1, Pallas kernels, per_device(): pl.pallas_call(hand_over, out_shape=tuple((shape(x.shape, F32) for x in (...  2.17 us

profile of v9, /device:TPU:1, one launch (start us, length us, event | category | flops | bytes accessed | tf_op | source)
XLA Modules:
  0.0 84.8 jit_solution(15165847986901035332)
XLA Ops:
  0.6 82.0 %gradient.1 = (f32[8,8,4,1024]{3,2,1,0:T(4,128)}, f32[8,4,1024]{2,1,0:T(4,128)}, f32[32,128]{1,0:T(8,128)}) custom-call(f32[8,8,4,1024]{3,2,1,0:T(4,128)} %ctl_hbm.1, f32[8,4,1024]{2,1,0:T(4,128)} %stc_hbm.1, bf16[2,8,8,4,1024]{4,3,2,1,0:T(4,128)(2,1)} %per_hbm.1, f32[8]{0:T(128)} %sigma_hbm.1, s32[4,1024]{1,0:T(4,128)} %cls_hbm.1, f32[4,1024]{1,0:T(4,128)} %east_hbm.1, ...), custom_call_target="tpu_custom_call" | custom-call | tf_op jit(solution)/shard_map/gradient/pallas_call | solution.py:809
  82.6 2.2 %results.1 = (f32[8,8,4,1024]{3,2,1,0:T(4,128)}, f32[8,4,1024]{2,1,0:T(4,128)}, f32[32,128]{1,0:T(8,128)}) custom-call(f32[8,8,4,1024]{3,2,1,0:T(4,128)} %get-tuple-element.9.x0, f32[8,4,1024]{2,1,0:T(4,128)} %get-tuple-element.10.x1, f32[32,128]{1,0:T(8,128)} %get-tuple-element.11.x2), custom_call_target="tpu_custom_call" | custom-call | tf_op jit(solution)/shard_map/results/pallas_call | solution.py:837

commit v10 on v9

--- a/solution.py
+++ b/solution.py
@@ -324,9 +324,9 @@
         value = turn(value, shift, True)
         if q == lev:
             value = jnp.where(usable, value, -1.0)
-        obs_s[:, q, :] = value
-    for q in range(lev + 3, 2 * lev):
-        obs_s[:, q, :] = jnp.zeros((group, LANES), F32)
+        obs_s[:, q // rows, q % rows, :] = value
+    for q in range(lev + 3, lev + rows):
+        obs_s[:, q // rows, q % rows, :] = jnp.zeros((group, LANES), F32)
 
     def obs_copy(j, d):
         return remote(
@@ -459,9 +459,19 @@
 
     chunks = ny
 
-    def lines_of(g, i, n=1):
+    def lines_of(g, i):
+        at = i % rows
         return jnp.concatenate(
-            [obs_r[g, j, i : i + n, :] for j in range(group)], axis=1
+            [obs_r[g, j, i // rows, at : at + 1, :] for j in range(group)], axis=1
+        )
+
+    def kernel_of(g):
+        return jnp.concatenate(
+            [
+                jnp.concatenate([obs_r[g, j, k] for k in range(lev // rows)], axis=0)
+                for j in range(group)
+            ],
+            axis=1,
         )
 
     lo_iota = lax.broadcasted_iota(jnp.int32, (LANES, group * LANES), 0)
@@ -472,7 +482,7 @@
         block = (col // LANES) & (ens - 1)
         unit = jnp.where((col >= 0) & (block == e), col // width, -1)
         himask[g] = jnp.broadcast_to(unit, (lev, group * LANES))
-        okern[g] = lines_of(g, 0, lev)
+        okern[g] = kernel_of(g)
         oaux[g, 0:1, :] = lines_of(g, lev + 1)
         oaux[g, 1:2, :] = lines_of(g, lev + 2)
         onehot[g] = jnp.where(
@@ -774,8 +784,8 @@
         vmem(hi_n, lev, width),
         vmem(ens, hi_n, lev, LANES),
         vmem(ens, hi_n, lev, LANES),
-        vmem(group, 2 * lev, LANES),
-        vmem(ny, group, 2 * lev, LANES),
+        vmem(group, lev // rows + 1, rows, LANES),
+        vmem(ny, group, lev // rows + 1, rows, LANES),
         vmem(chunks, LANES, slots, dtype=BF16),
         vmem(chunks, lev, slots, dtype=jnp.int32),
         vmem(chunks, lev, slots),

time: 84.9 us -> 84.6 us (level)
  no operation moved by 1% of the time
where the time goes in v10:
time: 84.6 us; the launch traced here: 84.4 us
  Pallas kernels  83.8 us (99%)
    pallas_call x1, Pallas kernels, per_device(): pl.pallas_call(functools.partial(kernel, factor, ens, tiles), out_shape=(...  81.6 us
    pallas_call x1, Pallas kernels, per_device(): pl.pallas_call(hand_over, out_shape=tuple((shape(x.shape, F32) for x in (...  2.17 us

profile of v10, /device:TPU:1, one launch (start us, length us, event | category | flops | bytes accessed | tf_op | source)
XLA Modules:
  0.0 84.4 jit_solution(18086992983557324030)
XLA Ops:
  0.6 81.6 %gradient.1 = (f32[8,8,4,1024]{3,2,1,0:T(4,128)}, f32[8,4,1024]{2,1,0:T(4,128)}, f32[32,128]{1,0:T(8,128)}) custom-call(f32[8,8,4,1024]{3,2,1,0:T(4,128)} %ctl_hbm.1, f32[8,4,1024]{2,1,0:T(4,128)} %stc_hbm.1, bf16[2,8,8,4,1024]{4,3,2,1,0:T(4,128)(2,1)} %per_hbm.1, f32[8]{0:T(128)} %sigma_hbm.1, s32[4,1024]{1,0:T(4,128)} %cls_hbm.1, f32[4,1024]{1,0:T(4,128)} %east_hbm.1, ...), custom_call_target="tpu_custom_call" | custom-call | tf_op jit(solution)/shard_map/gradient/pallas_call | solution.py:819
  82.3 2.2 %results.1 = (f32[8,8,4,1024]{3,2,1,0:T(4,128)}, f32[8,4,1024]{2,1,0:T(4,128)}, f32[32,128]{1,0:T(8,128)}) custom-call(f32[8,8,4,1024]{3,2,1,0:T(4,128)} %get-tuple-element.9.x0, f32[8,4,1024]{2,1,0:T(4,128)} %get-tuple-element.10.x1, f32[32,128]{1,0:T(8,128)} %get-tuple-element.11.x2), custom_call_target="tpu_custom_call" | custom-call | tf_op jit(solution)/shard_map/results/pallas_call | solution.py:847
